TPU v7x, 32 devices: a whole 2x2x4 slice. The times are simulated.
32 devices in a mesh: dp: 4 (over z), row: 2 (over x), col: 4 (over y, core).
Axes of the slice: x: 2, y: 2, z: 4, core: 2. Of those that a mesh axis runs over, the one named last changes fastest.
Arguments:
- tokens: bfloat16 [8, 256, 768], P('dp', None, 'row'), may hold values from -6 to 6
- condition: bfloat16 [8, 768], P('dp', 'col'), may hold values from -5 to 5
- cotangent: bfloat16 [8, 256, 768], P('dp', None, 'row'), may hold values from -6 to 6
- w_ada: bfloat16 [2, 768, 6, 768], P(None, 'col', None, 'row'), may hold values from -0.21875 to 0.21875
- b_ada: bfloat16 [2, 6, 768], P(None, None, 'row'), may hold values from -1.5 to 1.5
- w_qkv: bfloat16 [2, 768, 3, 768], P(None, 'row', None, 'col'), may hold values from -0.21875 to 0.21875
- b_qv: bfloat16 [2, 2, 768], P(None, None, 'col'), may hold values from -1.5 to 1.5
- w_out: bfloat16 [2, 768, 768], P(None, 'col', 'row'), may hold values from -1.75 to 1.75
- b_out: bfloat16 [2, 768], P(None, 'row'), may hold values from -1.5 to 1.5
- up_weight: bfloat16 [2, 768, 3072], P(None, 'row', 'col'), may hold values from -0.21875 to 0.21875
- up_bias: bfloat16 [2, 3072], P(None, 'col'), may hold values from -1.5 to 1.5
- down_weight: bfloat16 [2, 3072, 768], P(None, 'col', 'row'), may hold values from -0.109375 to 0.109375
- down_bias: bfloat16 [2, 768], P(None, 'row'), may hold values from -1.5 to 1.5
Outputs:
- result: bfloat16 [8, 256, 768], P('dp', None, 'row')
- tokens_grad: bfloat16 [8, 256, 768], P('dp', None, 'row')
- condition_grad: bfloat16 [8, 768], P('dp', 'col')
- w_ada_grad: float32 [2, 768, 6, 768], P(None, 'col', None, 'row')
- b_ada_grad: float32 [2, 6, 768], P(None, None, 'row')
- w_qkv_grad: float32 [2, 768, 3, 768], P(None, 'row', None, 'col')
- b_qv_grad: float32 [2, 2, 768], P(None, None, 'col')
- w_out_grad: float32 [2, 768, 768], P(None, 'col', 'row')
- b_out_grad: float32 [2, 768], P(None, 'row')
- w_up_grad: float32 [2, 768, 3072], P(None, 'row', 'col')
- b_up_grad: float32 [2, 3072], P(None, 'col')
- w_down_grad: float32 [2, 3072, 768], P(None, 'col', 'row')
- b_down_grad: float32 [2, 768], P(None, 'row')
All inputs are finite; a program needn't handle non-finite values.
Results may differ from a plain program's by a relative error of at most 0.025.
Values may be sent and summed in bfloat16 or wider, within the bound.
A program may use at most 128 MiB of HBM per device.

v0:
```python
import jax
import jax.numpy as jnp
from jax import lax
from jax.sharding import PartitionSpec as P

HEAD = 64


EPSILON = 1e-06


def silu_plain(values):
    return values * jax.nn.sigmoid(values)


def gelu_tanh(values):
    return (
        0.5
        * values
        * (1.0 + jnp.tanh(0.7978845608028654 * (values + 0.044715 * values * values * values)))
    )


def row_moments(first_terms, second_terms):
    first_sum = jnp.sum(first_terms, axis=-1, keepdims=True)
    second_sum = jnp.sum(second_terms, axis=-1, keepdims=True)
    first_sum, second_sum = lax.psum((first_sum, second_sum), "row")
    full_width = first_terms.shape[-1] * lax.axis_size("row")
    return (first_sum / full_width, second_sum / full_width)


def normalize(stream):
    average, square = row_moments(stream, stream * stream)
    inverse = lax.rsqrt(square - average * average + EPSILON)
    return ((stream - average) * inverse, inverse)


def norm_back(grad_norm, normed, inverse):
    first_mean, second_mean = row_moments(grad_norm, grad_norm * normed)
    return inverse * (grad_norm - first_mean - normed * second_mean)


def over_row(term_maker, latents):
    return lax.psum_scatter(
        term_maker(jnp.int32(0), latents // lax.axis_size("row") * lax.axis_size("row")),
        "row",
        scatter_dimension=0,
        tiled=True,
    )


def to_all_rows(pieces):
    return lax.all_gather(pieces, "row", axis=0, tiled=True)


def over_col(term):
    return lax.psum(term.astype(jnp.bfloat16), "col").astype(jnp.float32)


def split_heads(projected):
    head_view = projected.reshape(projected.shape[0], projected.shape[1], 3, -1, HEAD)
    return (head_view[:, :, 0], head_view[:, :, 1], head_view[:, :, 2])


def attention_forward(projected):
    queries, key_rows, value_rows = split_heads(projected)
    scores = jnp.einsum(
        "lqhe,lkhe->lhqk", queries, key_rows, preferred_element_type=jnp.float32
    ) * HEAD ** (-0.5)
    highest = jnp.max(scores, axis=-1, keepdims=True)
    expos = jnp.exp(scores - highest)
    totals = jnp.sum(expos, axis=-1, keepdims=True)
    soft_low = (expos / totals).astype(jnp.bfloat16)
    head_mix = jnp.einsum(
        "lhqk,lkhe->lqhe", soft_low, value_rows, preferred_element_type=jnp.float32
    )
    shaped = head_mix.reshape(projected.shape[0], projected.shape[1], -1).astype(jnp.bfloat16)
    return (shaped, highest + jnp.log(totals))


def attention_backward(projected, log_totals, grad_mix):
    queries, key_rows, value_rows = split_heads(projected)
    scale_factor = HEAD ** (-0.5)
    scores = (
        jnp.einsum("lqhe,lkhe->lhqk", queries, key_rows, preferred_element_type=jnp.float32)
        * scale_factor
    )
    weights_soft = jnp.exp(scores - log_totals)
    grad_heads = grad_mix.reshape(grad_mix.shape[0], grad_mix.shape[1], -1, HEAD)
    grad_soft = jnp.einsum(
        "lqhe,lkhe->lhqk", grad_heads, value_rows, preferred_element_type=jnp.float32
    )
    grad_values = jnp.einsum(
        "lhqk,lqhe->lkhe",
        weights_soft.astype(jnp.bfloat16),
        grad_heads,
        preferred_element_type=jnp.float32,
    )
    grad_scores = weights_soft * (
        grad_soft - jnp.sum(weights_soft * grad_soft, axis=-1, keepdims=True)
    )
    grad_scores = grad_scores.astype(jnp.bfloat16)
    grad_queries = (
        jnp.einsum("lhqk,lkhe->lqhe", grad_scores, key_rows, preferred_element_type=jnp.float32)
        * scale_factor
    )
    grad_keys = (
        jnp.einsum("lhqk,lqhe->lkhe", grad_scores, queries, preferred_element_type=jnp.float32)
        * scale_factor
    )
    stacked = jnp.stack([grad_queries, grad_keys, grad_values], axis=2)
    return stacked.reshape(projected.shape).astype(jnp.bfloat16)


def local(
    tokens,
    condition,
    cotangent,
    w_ada,
    b_ada,
    w_qkv,
    b_qv,
    w_out,
    b_out,
    up_weight,
    up_bias,
    down_weight,
    down_bias,
):
    layers = w_ada.shape[0]
    cond_float = condition.astype(jnp.float32)
    latents = tokens.shape[0]
    cond_low = silu_plain(cond_float).astype(jnp.bfloat16)
    modulation = lax.psum(
        jnp.einsum("lc,nckd->nlkd", cond_low, w_ada, preferred_element_type=jnp.float32), "col"
    )
    modulation = modulation + b_ada.astype(jnp.float32)[:, None]
    stream = tokens.astype(jnp.float32)
    kept_state = []
    for layer_position in range(layers):
        mod_parts = modulation[layer_position]
        shift_one, scale_one, gate_one, shift_two, scale_two, gate_two = [
            mod_parts[:, slot_index][:, None, :] for slot_index in range(6)
        ]
        normed_one, inverse_one = normalize(stream)
        hidden_one = (normed_one * (1.0 + scale_one) + shift_one).astype(jnp.bfloat16)
        weight_qkv = w_qkv[layer_position]
        bias_pair = b_qv[layer_position].astype(jnp.float32)
        bias_three = jnp.stack([bias_pair[0], jnp.zeros_like(bias_pair[0]), bias_pair[1]])

        def make_qkv(first_row, row_count):
            return jnp.einsum(
                "lsd,dke->lske", hidden_one, weight_qkv, preferred_element_type=jnp.float32
            )

        projected = (over_row(make_qkv, latents) + bias_three).astype(jnp.bfloat16)
        head_mix, log_totals = attention_forward(projected)
        mix_all = to_all_rows(head_mix)
        attention = over_col(
            jnp.einsum(
                "lsc,cd->lsd", mix_all, w_out[layer_position], preferred_element_type=jnp.float32
            )
        )
        attention = attention + b_out[layer_position].astype(jnp.float32)
        after_attn = stream + gate_one * attention
        normed_two, inverse_two = normalize(after_attn)
        second_hidden = (normed_two * (1.0 + scale_two) + shift_two).astype(jnp.bfloat16)
        up_weight_block = up_weight[layer_position]

        def make_up(first_row, row_count):
            return jnp.einsum(
                "zha,aw->zhw", second_hidden, up_weight_block, preferred_element_type=jnp.float32
            )

        before_feed = over_row(make_up, latents) + up_bias[layer_position].astype(jnp.float32)
        activated_hidden = gelu_tanh(before_feed).astype(jnp.bfloat16)
        activation_gathered = to_all_rows(activated_hidden)
        feed_output = over_col(
            jnp.einsum(
                "pqc,ct->pqt",
                activation_gathered,
                down_weight[layer_position],
                preferred_element_type=jnp.float32,
            )
        )
        feed_output = feed_output + down_bias[layer_position].astype(jnp.float32)
        kept_state.append(
            (
                normed_one,
                inverse_one,
                hidden_one,
                projected,
                log_totals,
                mix_all,
                attention,
                normed_two,
                inverse_two,
                second_hidden,
                before_feed,
                activation_gathered,
                feed_output,
            )
        )
        stream = after_attn + gate_two * feed_output
    result = stream.astype(jnp.bfloat16)
    grad_stream = cotangent.astype(jnp.float32)
    cond_term = jnp.zeros(cond_float.shape, jnp.float32)
    layer_sums = [None] * layers
    for layer_position in reversed(range(layers)):
        (
            normed_one,
            inverse_one,
            hidden_one,
            projected,
            log_totals,
            mix_all,
            attention,
            normed_two,
            inverse_two,
            second_hidden,
            before_feed,
            activation_gathered,
            feed_output,
        ) = kept_state[layer_position]
        mod_parts = modulation[layer_position]
        shift_one, scale_one, gate_one, shift_two, scale_two, gate_two = [
            mod_parts[:, slot_index][:, None, :] for slot_index in range(6)
        ]
        grad_gate_two = jnp.sum(grad_stream * feed_output, axis=1)
        feed_gradient = (grad_stream * gate_two).astype(jnp.bfloat16)
        grad_b_down = jnp.sum(feed_gradient, axis=(0, 1), dtype=jnp.float32)
        grad_w_down = jnp.einsum(
            "kju,kje->ue", activation_gathered, feed_gradient, preferred_element_type=jnp.float32
        )
        down_weight_block = down_weight[layer_position]

        def make_act(first_row, row_count):
            return jnp.einsum(
                "evn,cn->evc", feed_gradient, down_weight_block, preferred_element_type=jnp.float32
            )

        grad_act = over_row(make_act, latents)
        gelu_pull = jax.vjp(gelu_tanh, before_feed)[1]
        grad_before = gelu_pull(grad_act)[0].astype(jnp.bfloat16)
        gradient_before_gathered = to_all_rows(grad_before)
        grad_b_up = jnp.sum(gradient_before_gathered, axis=(0, 1), dtype=jnp.float32)
        grad_w_up = jnp.einsum(
            "rak,raw->kw",
            second_hidden,
            gradient_before_gathered,
            preferred_element_type=jnp.float32,
        )
        grad_hidden_two = over_col(
            jnp.einsum(
                "jqp,np->jqn",
                gradient_before_gathered,
                up_weight[layer_position],
                preferred_element_type=jnp.float32,
            )
        )
        grad_scale_two = jnp.sum(grad_hidden_two * normed_two, axis=1)
        grad_shift_two = jnp.sum(grad_hidden_two, axis=1)
        grad_mid = grad_stream + norm_back(
            grad_hidden_two * (1.0 + scale_two), normed_two, inverse_two
        )
        grad_gate_one = jnp.sum(grad_mid * attention, axis=1)
        grad_attn = (grad_mid * gate_one).astype(jnp.bfloat16)
        grad_b_out = jnp.sum(grad_attn, axis=(0, 1), dtype=jnp.float32)
        grad_w_out = jnp.einsum(
            "lsc,lsd->cd", mix_all, grad_attn, preferred_element_type=jnp.float32
        )
        weight_out = w_out[layer_position]

        def make_mix(first_row, row_count):
            return jnp.einsum(
                "lsd,cd->lsc", grad_attn, weight_out, preferred_element_type=jnp.float32
            )

        grad_mix = over_row(make_mix, latents).astype(jnp.bfloat16)
        grad_projected = attention_backward(projected, log_totals, grad_mix)
        grad_proj_all = to_all_rows(grad_projected)
        three_sums = jnp.sum(grad_proj_all, axis=(0, 1), dtype=jnp.float32)
        grad_b_qv = jnp.stack([three_sums[0], three_sums[2]])
        grad_w_qkv = jnp.einsum(
            "lsd,lske->dke", hidden_one, grad_proj_all, preferred_element_type=jnp.float32
        )
        grad_hidden_one = over_col(
            jnp.einsum(
                "lske,dke->lsd",
                grad_proj_all,
                w_qkv[layer_position],
                preferred_element_type=jnp.float32,
            )
        )
        grad_scale_one = jnp.sum(grad_hidden_one * normed_one, axis=1)
        grad_shift_one = jnp.sum(grad_hidden_one, axis=1)
        grad_stream = grad_mid + norm_back(
            grad_hidden_one * (1.0 + scale_one), normed_one, inverse_one
        )
        grad_mod = jnp.stack(
            [
                grad_shift_one,
                grad_scale_one,
                grad_gate_one,
                grad_shift_two,
                grad_scale_two,
                grad_gate_two,
            ],
            axis=1,
        )
        grad_mod = grad_mod.astype(jnp.bfloat16)
        grad_b_ada = jnp.sum(grad_mod, axis=0, dtype=jnp.float32)
        grad_w_ada = jnp.einsum(
            "lc,lkd->ckd", cond_low, grad_mod, preferred_element_type=jnp.float32
        )
        cond_term = cond_term + jnp.einsum(
            "lkd,ckd->lc", grad_mod, w_ada[layer_position], preferred_element_type=jnp.float32
        )
        layer_sums[layer_position] = (
            grad_w_ada,
            grad_b_ada,
            grad_w_qkv,
            grad_b_qv,
            grad_w_out,
            grad_b_out,
            grad_w_up,
            grad_b_up,
            grad_w_down,
            grad_b_down,
        )
    cond_sum = lax.psum(cond_term, "row")
    condition_grad = jax.vjp(silu_plain, cond_float)[1](cond_sum)[0].astype(jnp.bfloat16)
    stacked = [
        jnp.stack([layer_sums[layer_position][position] for layer_position in range(layers)])
        for position in range(10)
    ]
    stacked = (
        lax.psum(stacked[0].astype(jnp.bfloat16), "dp").astype(jnp.float32),
        lax.psum(stacked[1].astype(jnp.bfloat16), "dp").astype(jnp.float32),
        lax.psum(stacked[2].astype(jnp.bfloat16), "dp").astype(jnp.float32),
        lax.psum(stacked[3].astype(jnp.bfloat16), "dp").astype(jnp.float32),
        lax.psum(stacked[4].astype(jnp.bfloat16), "dp").astype(jnp.float32),
        lax.psum(stacked[5].astype(jnp.bfloat16), "dp").astype(jnp.float32),
        lax.psum(stacked[6].astype(jnp.bfloat16), "dp").astype(jnp.float32),
        lax.psum(stacked[7].astype(jnp.bfloat16), "dp").astype(jnp.float32),
        lax.psum(stacked[8].astype(jnp.bfloat16), "dp").astype(jnp.float32),
        lax.psum(stacked[9].astype(jnp.bfloat16), "dp").astype(jnp.float32),
    )
    grad_out = grad_stream.astype(jnp.bfloat16)
    return (
        result,
        grad_out,
        condition_grad,
        stacked[0],
        stacked[1],
        stacked[2],
        stacked[3],
        stacked[4],
        stacked[5],
        stacked[6],
        stacked[7],
        stacked[8],
        stacked[9],
    )


def solution(mesh):
    in_specs = (
        P("dp", None, "row"),
        P("dp", "col"),
        P("dp", None, "row"),
        P(None, "col", None, "row"),
        P(None, None, "row"),
        P(None, "row", None, "col"),
        P(None, None, "col"),
        P(None, "col", "row"),
        P(None, "row"),
        P(None, "row", "col"),
        P(None, "col"),
        P(None, "col", "row"),
        P(None, "row"),
    )
    out_specs = (
        P("dp", None, "row"),
        P("dp", None, "row"),
        P("dp", "col"),
        P(None, "col", None, "row"),
        P(None, None, "row"),
        P(None, "row", None, "col"),
        P(None, None, "col"),
        P(None, "col", "row"),
        P(None, "row"),
        P(None, "row", "col"),
        P(None, "col"),
        P(None, "col", "row"),
        P(None, "row"),
    )
    return jax.shard_map(local, mesh=mesh, in_specs=in_specs, out_specs=out_specs, check_vma=False)
```

profile of v0, /device:TPU:0, one launch (start us, length us, event | category | flops | bytes accessed | tf_op | source)
XLA Modules:
  0.0 815.7 jit_solution(10419982153252050957)
XLA Ops:
  11.1 13.2 %psum.252 = f32[2,2,6,384]{3,1,2,0:T(2,128)S(1)} all-reduce(f32[2,2,6,384]{3,1,2,0:T(2,128)S(1)} %convolution_bitcast_fusion.10), channel_id=1, replica_groups=mesh['dp'=4,'row'=2,'col'=4] {'col'}, use_global_device_ids=true, to_apply=%region_0.0 | all-reduce | flops 9216 | bytes 73728 | tf_op jit(solution)/shard_map/psum | solution.py:134
  25.5 4.9 all-reduce.7
  33.1 21.4 %reduce-scatter.9.cloned.1.call-done = f32[1,256,3,192]{1,3,2,0:T(8,128)} async-done(((f32[2,256,3,192]{1,3,2,0:T(8,128)}), f32[1,256,3,192]{1,3,2,0:T(8,128)}) %reduce-scatter.9.cloned.1.call-update) | async-done | bytes 589840 | tf_op jit(solution)/shard_map/reduce_scatter | solution.py:44
  56.7 5.4 all_gather.24
  63.9 32.1 %all-reduce.20.cloned.1.call-done = bf16[2,256,384]{2,1,0:T(8,128)(2,1)} async-done(((bf16[2,256,384]{2,1,0:T(8,128)(2,1)}), bf16[2,256,384]{2,1,0:T(8,128)(2,1)}) %all-reduce.20.cloned.1.call-update) | async-done | bytes 393232 | tf_op jit(solution)/shard_map/psum | solution.py:57
  97.3 4.9 all-reduce.6
  102.3 2.8 fusion.95
  107.0 24.4 %reduce-scatter.11.cloned.1.call-done = f32[1,256,768]{2,1,0:T(8,128)} async-done(((f32[2,256,768]{2,1,0:T(8,128)}), f32[1,256,768]{2,1,0:T(8,128)}) %reduce-scatter.11.cloned.1.call-update) | async-done | bytes 786448 | tf_op jit(solution)/shard_map/reduce_scatter | solution.py:44
  132.9 11.5 %all_gather.25 = bf16[2,256,768]{2,1,0:T(8,128)(2,1)S(1)} all-gather(bf16[1,256,768]{2,1,0:T(8,128)(2,1)S(1)} %multiply_convert_fusion.6), channel_id=1, replica_groups=mesh['dp'=4,'row'=2,'col'=4] {'row'}, dimensions={0}, use_global_device_ids=true | all-gather | bytes 1179648 | tf_op jit(solution)/shard_map/all_gather | solution.py:53
  147.2 31.4 %all-reduce.22.cloned.1.call-done = bf16[2,256,384]{2,1,0:T(8,128)(2,1)} async-done(((bf16[2,256,384]{2,1,0:T(8,128)(2,1)}), bf16[2,256,384]{2,1,0:T(8,128)(2,1)}) %all-reduce.22.cloned.1.call-update) | async-done | bytes 393232 | tf_op jit(solution)/shard_map/psum | solution.py:57
  180.0 4.9 all-reduce.5
  185.0 2.7 fusion.106
  187.8 21.9 %reduce-scatter.13.cloned.1.call-done = f32[1,256,3,192]{1,3,2,0:T(8,128)} async-done(((f32[2,256,3,192]{1,3,2,0:T(8,128)}), f32[1,256,3,192]{1,3,2,0:T(8,128)}) %reduce-scatter.13.cloned.1.call-update) | async-done | bytes 589840 | tf_op jit(solution)/shard_map/reduce_scatter | solution.py:44
  212.2 5.4 all_gather.26
  218.7 2.8 fusion.85
  221.6 29.8 %all-reduce.24.cloned.1.call-done = bf16[2,256,384]{2,1,0:T(8,128)(2,1)} async-done(((bf16[2,256,384]{2,1,0:T(8,128)(2,1)}), bf16[2,256,384]{2,1,0:T(8,128)(2,1)}) %all-reduce.24.cloned.1.call-update) | async-done | bytes 393232 | tf_op jit(solution)/shard_map/psum | solution.py:57
  253.3 5.6 all-reduce.4
  260.2 2.9 fusion.89
  263.2 17.1 %reduce-scatter.17.cloned.1.call-done = f32[1,256,768]{2,1,0:T(8,128)} async-done(((f32[2,256,768]{2,1,0:T(8,128)}), f32[1,256,768]{2,1,0:T(8,128)}) %reduce-scatter.17.cloned.1.call-update) | async-done | bytes 786448 | tf_op jit(solution)/shard_map/reduce_scatter | solution.py:44
  280.4 29.0 %reduce-scatter.15.cloned.1.call-done = f32[1,256,768]{2,1,0:T(8,128)} async-done(((f32[2,256,768]{2,1,0:T(8,128)}), f32[1,256,768]{2,1,0:T(8,128)}) %reduce-scatter.15.cloned.1.call-update) | async-done | bytes 786448 | tf_op jit(solution)/shard_map/reduce_scatter | solution.py:44
  309.4 2.8 fusion.68
  312.2 11.7 %all_gather.28 = bf16[2,256,768]{2,1,0:T(8,128)(2,1)S(1)} all-gather(bf16[1,256,768]{2,1,0:T(8,128)(2,1)S(1)} %get-tuple-element.105), channel_id=1, replica_groups=mesh['dp'=4,'row'=2,'col'=4] {'row'}, dimensions={0}, use_global_device_ids=true | all-gather | bytes 1179648 | tf_op jit(solution)/shard_map/all_gather | solution.py:53
  326.2 32.7 %all-reduce.26.cloned.1.call-done = bf16[2,256,384]{2,1,0:T(8,128)(2,1)} async-done(((bf16[2,256,384]{2,1,0:T(8,128)(2,1)}), bf16[2,256,384]{2,1,0:T(8,128)(2,1)}) %all-reduce.26.cloned.1.call-update) | async-done | bytes 393232 | tf_op jit(solution)/shard_map/psum | solution.py:57
  361.0 5.6 all-reduce.3
  368.0 3.3 fusion.164
  374.0 12.3 %reduce-scatter.19.cloned.1.call-done = f32[1,256,192]{1,2,0:T(8,128)} async-done(((f32[2,256,192]{1,2,0:T(8,128)}), f32[1,256,192]{1,2,0:T(8,128)}) %reduce-scatter.19.cloned.1.call-update) | async-done | bytes 196624 | tf_op jit(solution)/shard_map/reduce_scatter | solution.py:44
  388.6 9.7 %all_gather.29 = bf16[2,256,3,192]{1,3,2,0:T(8,128)(2,1)} all-gather(bf16[1,256,3,192]{1,3,2,0:T(8,128)(2,1)S(1)} %pad_maximum_fusion.4), channel_id=1, replica_groups=mesh['dp'=4,'row'=2,'col'=4] {'row'}, dimensions={0}, use_global_device_ids=true | all-gather | bytes 884736 | tf_op jit(solution)/shard_map/all_gather | solution.py:53
  398.3 2.4 fusion.8
  400.8 32.7 %all-reduce.28.cloned.1.call-done = bf16[2,256,384]{2,1,0:T(8,128)(2,1)} async-done(((bf16[2,256,384]{2,1,0:T(8,128)(2,1)}), bf16[2,256,384]{2,1,0:T(8,128)(2,1)}) %all-reduce.28.cloned.1.call-update) | async-done | bytes 393232 | tf_op jit(solution)/shard_map/psum | solution.py:57
  435.6 5.6 all-reduce.2
  442.6 3.0 fusion.160
  449.6 15.9 %all_gather.27 = bf16[2,256,768]{2,1,0:T(8,128)(2,1)S(1)} all-gather(bf16[1,256,768]{2,1,0:T(8,128)(2,1)} %get-tuple-element.106), channel_id=1, replica_groups=mesh['dp'=4,'row'=2,'col'=4] {'row'}, dimensions={0}, use_global_device_ids=true | all-gather | bytes 1179648 | tf_op jit(solution)/shard_map/all_gather | solution.py:53
  471.0 2.5 fusion.14
  473.6 3.3 reduce-scatter.21.cloned.1.call-done
  478.8 11.7 %all_gather.30 = bf16[2,256,768]{2,1,0:T(8,128)(2,1)S(1)} all-gather(bf16[1,256,768]{2,1,0:T(8,128)(2,1)S(1)} %fusion.64), channel_id=1, replica_groups=mesh['dp'=4,'row'=2,'col'=4] {'row'}, dimensions={0}, use_global_device_ids=true | all-gather | bytes 1179648 | tf_op jit(solution)/shard_map/all_gather | solution.py:53
  495.3 30.3 %all-reduce.30.cloned.1.call-done = bf16[2,256,384]{2,1,0:T(8,128)(2,1)} async-done(((bf16[2,256,384]{2,1,0:T(8,128)(2,1)}), bf16[2,256,384]{2,1,0:T(8,128)(2,1)}) %all-reduce.30.cloned.1.call-update) | async-done | bytes 393232 | tf_op jit(solution)/shard_map/psum | solution.py:57
  525.6 2.1 fusion.54
  527.7 4.9 all-reduce.1
  532.6 2.5 fusion.162
  536.3 2.5 pad_maximum_fusion.2
  542.6 6.9 reduce-scatter.23.cloned.1.call-done
  551.8 9.6 %all_gather.31 = bf16[2,256,3,192]{1,3,2,0:T(8,128)(2,1)S(1)} all-gather(bf16[1,256,3,192]{1,3,2,0:T(8,128)(2,1)S(1)} %pad_maximum_fusion.5), channel_id=1, replica_groups=mesh['dp'=4,'row'=2,'col'=4] {'row'}, dimensions={0}, use_global_device_ids=true | all-gather | bytes 884736 | tf_op jit(solution)/shard_map/all_gather | solution.py:53
  565.8 31.8 %all-reduce.32.cloned.1.call-done = (bf16[2,256,384]{2,1,0:T(8,128)(2,1)}, bf16[2,256,384]{2,1,0:T(8,128)(2,1)}) async-done(((bf16[2,256,384]{2,1,0:T(8,128)(2,1)}, bf16[2,256,384]{2,1,0:T(8,128)(2,1)}), (bf16[2,256,384]{2,1,0:T(8,128)(2,1)}, bf16[2,256,384]{2,1,0:T(8,128)(2,1)})) %all-reduce.32.cloned.1.call-update) | async-done | bytes 786448 | tf_op jit(solution)/shard_map/psum | solution.py:57
  597.6 2.1 fusion.60
  610.5 21.7 %all-reduce.9 = (bf16[2,6,384]{2,1,0:T(8,128)(2,1)S(1)}, bf16[2,2,192]{2,1,0:T(2,128)(2,1)S(1)}, bf16[2,384]{1,0:T(2,128)(2,1)S(1)}, bf16[2,768]{1,0:T(2,128)(2,1)S(1)}, bf16[2,384]{1,0:T(2,128)(2,1)S(1)}) all-reduce(bf16[2,6,384]{2,1,0:T(8,128)(2,1)S(1)} %pad_maximum_fusion.7, ...), channel_id=1, replica_groups=mesh['dp'=4,'row'=2,'col'=4] {'dp'}, use_global_device_ids=true, to_apply=%region_71.0 | all-reduce | flops 8448 | bytes 33792 | tf_op jit(solution)/shard_map/psum | solution.py:339
  635.9 5.0 all-reduce
  642.6 156.0 %all-reduce.34.cloned.1.call-done = (bf16[2,192,6,384]{3,1,2,0:T(8,128)(2,1)}, bf16[2,384,3,192]{1,3,2,0:T(8,128)(2,1)}, bf16[2,192,384]{2,1,0:T(8,128)(2,1)}, b...) async-done(((bf16[2,192,6,384]{3,1,2,0:T(8,128)(2,1)}, bf16[2,384,3,192]{1,3,2,0:T(8,128)(2,1)}, bf16[2,192,384]{2,1,0:T(8,128)(2,1)}, bf16[2,384,768]{2,1,0:T(8,128)(2,1)}, ...) | async-done | bytes 5308432 | tf_op jit(solution)/shard_map/psum | solution.py:338
  800.4 3.7 convert_element_type.410
  (412 shorter events, 91.8 us)
Async XLA Ops:
  7.2 47.2 %reduce-scatter.9.cloned.1.call-start = ((), (), s32[]{:S(2)}) async-start(), calls=%async_computation.8 | async-start | bytes 1769472 | tf_op jit(solution)/shard_map/reduce_scatter | solution.py:44
  25.5 76.8 %copy-start.76 = (f32[2,384]{1,0:T(2,128)}, f32[2,384]{1,0:T(2,128)S(1)}, u32[]{:S(2)}) copy-start(f32[2,384]{1,0:T(2,128)S(1)} %get-tuple-element.123) | copy-start | bytes 9220
  25.5 76.8 %copy-start.121 = (f32[2,384]{1,0:T(2,128)}, f32[2,384]{1,0:T(2,128)S(1)}, u32[]{:S(2)}) copy-start(f32[2,384]{1,0:T(2,128)S(1)} %get-tuple-element.122) | copy-start | bytes 9220
  32.3 63.7 %all-reduce.20.cloned.1.call-start = ((), (), s32[]{:S(2)}) async-start(), calls=%async_computation.9 | async-start | bytes 786432 | tf_op jit(solution)/shard_map/psum | solution.py:57
  56.7 45.6 %copy-start.47 = (bf16[2,384,768]{2,1,0:T(8,128)(2,1)S(1)}, bf16[2,384,768]{2,1,0:T(8,128)(2,1)}, u32[]{:S(2)}) copy-start(bf16[2,384,768]{2,1,0:T(8,128)(2,1)} %param.22) | copy-start | bytes 3538948
  62.1 43.0 %copy-start.23 = (bf16[2,256,192]{1,2,0:T(8,128)(2,1)}, bf16[2,256,192]{1,2,0:T(8,128)(2,1)S(1)}, u32[]{:S(2)}) copy-start(bf16[2,256,192]{1,2,0:T(8,128)(2,1)S(1)} %all_gather.24) | copy-start | bytes 589828
  63.2 68.2 %reduce-scatter.11.cloned.1.call-start = ((), (), s32[]{:S(2)}) async-start(), calls=%async_computation.10 | async-start | bytes 2359296 | tf_op jit(solution)/shard_map/reduce_scatter | solution.py:44
  63.9 114.7 %copy-start.55 = (f32[384]{0:T(512)}, f32[384]{0:T(512)S(1)}, u32[]{:S(2)}) copy-start(f32[384]{0:T(512)S(1)} %get-tuple-element.64) | copy-start | bytes 4612
  105.2 73.4 %all-reduce.22.cloned.1.call-start = ((), (), s32[]{:S(2)}) async-start(), calls=%async_computation.11 | async-start | bytes 786432 | tf_op jit(solution)/shard_map/psum | solution.py:57
  107.0 37.4 %copy-start.64 = (f32[768]{0:T(1024)}, f32[768]{0:T(1024)S(1)}, u32[]{:S(2)}) copy-start(f32[768]{0:T(1024)S(1)} %get-tuple-element.60) | copy-start | bytes 9220
  144.5 34.1 %copy-start.1 = (bf16[2,256,384]{2,1,0:T(8,128)(2,1)S(1)}, bf16[2,256,384]{2,1,0:T(8,128)(2,1)}, u32[]{:S(2)}) copy-start(bf16[2,256,384]{2,1,0:T(8,128)(2,1)} %all-reduce.20.cloned.1.call-done) | copy-start | bytes 1179652
  145.8 63.8 %reduce-scatter.13.cloned.1.call-start = ((), (), s32[]{:S(2)}) async-start(), calls=%async_computation.12 | async-start | bytes 1769472 | tf_op jit(solution)/shard_map/reduce_scatter | solution.py:44
  147.2 40.4 %copy-start.61 = (f32[2,384]{1,0:T(2,128)}, f32[2,384]{1,0:T(2,128)S(1)}, u32[]{:S(2)}) copy-start(f32[2,384]{1,0:T(2,128)S(1)} %get-tuple-element.119) | copy-start | bytes 9220
  147.2 40.4 %copy-start.100 = (f32[2,384]{1,0:T(2,128)}, f32[2,384]{1,0:T(2,128)S(1)}, u32[]{:S(2)}) copy-start(f32[2,384]{1,0:T(2,128)S(1)} %get-tuple-element.118) | copy-start | bytes 9220
  147.2 318.3 %copy-start.59 = (f32[2,384]{1,0:T(2,128)}, f32[2,384]{1,0:T(2,128)S(1)}, u32[]{:S(2)}) copy-start(f32[2,384]{1,0:T(2,128)S(1)} %get-tuple-element.115) | copy-start | bytes 9220
  187.7 63.7 %all-reduce.24.cloned.1.call-start = ((), (), s32[]{:S(2)}) async-start(), calls=%async_computation.13 | async-start | bytes 786432 | tf_op jit(solution)/shard_map/psum | solution.py:57
  218.7 61.7 %reduce-scatter.17.cloned.1.call-start = ((), (), s32[]{:S(2)}) async-start(), calls=%async_computation.15 | async-start | bytes 2359296 | tf_op jit(solution)/shard_map/reduce_scatter | solution.py:44
  221.6 29.9 %copy-start.79 = (f32[2,384]{1,0:T(2,128)S(1)}, f32[2,384]{1,0:T(2,128)}, u32[]{:S(2)}) copy-start(f32[2,384]{1,0:T(2,128)} %get-tuple-element.120) | copy-start | bytes 9220
  221.6 87.8 %reduce-scatter.15.cloned.1.call-start = ((), (), s32[]{:S(2)}) async-start(), calls=%async_computation.14 | async-start | bytes 2359296 | tf_op jit(solution)/shard_map/reduce_scatter | solution.py:44
  259.6 108.3 %copy-start.66 = (f32[2,256]{1,0:T(2,128)}, f32[2,256]{1,0:T(2,128)S(1)}, u32[]{:S(2)}) copy-start(f32[2,256]{1,0:T(2,128)S(1)} %get-tuple-element.131) | copy-start | bytes 6148
  263.2 95.7 %all-reduce.26.cloned.1.call-start = ((), (), s32[]{:S(2)}) async-start(), calls=%async_computation.16 | async-start | bytes 786432 | tf_op jit(solution)/shard_map/psum | solution.py:57
  326.1 60.2 %reduce-scatter.19.cloned.1.call-start = ((), (), s32[]{:S(2)}) async-start(), calls=%async_computation.17 | async-start | bytes 589824 | tf_op jit(solution)/shard_map/reduce_scatter | solution.py:44
  373.1 60.4 %all-reduce.28.cloned.1.call-start = ((), (), s32[]{:S(2)}) async-start(), calls=%async_computation.18 | async-start | bytes 786432 | tf_op jit(solution)/shard_map/psum | solution.py:57
  398.3 35.2 %copy-start.62 = (f32[2,384]{1,0:T(2,128)S(1)}, f32[2,384]{1,0:T(2,128)}, u32[]{:S(2)}) copy-start(f32[2,384]{1,0:T(2,128)} %copy-done.61) | copy-start | bytes 9220
  400.7 41.9 %copy-start.4 = (f32[2,256,384]{2,1,0:T(8,128)S(1)}, f32[2,256,384]{2,1,0:T(8,128)}, u32[]{:S(2)}) copy-start(f32[2,256,384]{2,1,0:T(8,128)} %get-tuple-element.102) | copy-start | bytes 2359300
  400.8 76.2 %reduce-scatter.21.cloned.1.call-start = ((), (), s32[]{:S(2)}) async-start(), calls=%async_computation.19 | async-start | bytes 2359296 | tf_op jit(solution)/shard_map/reduce_scatter | solution.py:44
  448.2 77.4 %all-reduce.30.cloned.1.call-start = ((), (), s32[]{:S(2)}) async-start(), calls=%async_computation.20 | async-start | bytes 786432 | tf_op jit(solution)/shard_map/psum | solution.py:57
  490.6 42.0 %copy-start.15 = (bf16[2,256,768]{2,1,0:T(8,128)(2,1)}, bf16[2,256,768]{2,1,0:T(8,128)(2,1)S(1)}, u32[]{:S(2)}) copy-start(bf16[2,256,768]{2,1,0:T(8,128)(2,1)S(1)} %all_gather.30) | copy-start | bytes 2359300
  492.0 57.5 %reduce-scatter.23.cloned.1.call-start = ((), (), s32[]{:S(2)}) async-start(), calls=%async_computation.21 | async-start | bytes 589824 | tf_op jit(solution)/shard_map/reduce_scatter | solution.py:44
  493.8 31.7 %copy-start.2 = (bf16[2,256,384]{2,1,0:T(8,128)(2,1)S(1)}, bf16[2,256,384]{2,1,0:T(8,128)(2,1)}, u32[]{:S(2)}) copy-start(bf16[2,256,384]{2,1,0:T(8,128)(2,1)} %all-reduce.20.cloned.1.call-done) | copy-start | bytes 1179652
  493.8 31.7 %copy-start.56 = (f32[384]{0:T(512)S(1)}, f32[384]{0:T(512)}, u32[]{:S(2)}) copy-start(f32[384]{0:T(512)} %copy-done.55) | copy-start | bytes 4612
  493.8 31.7 %copy-start.77 = (f32[2,384]{1,0:T(2,128)S(1)}, f32[2,384]{1,0:T(2,128)}, u32[]{:S(2)}) copy-start(f32[2,384]{1,0:T(2,128)} %copy-done.76) | copy-start | bytes 9220
  493.8 31.7 %copy-start.82 = (f32[2,256]{1,0:T(2,128)S(1)}, f32[2,256]{1,0:T(2,128)}, u32[]{:S(2)}) copy-start(f32[2,256]{1,0:T(2,128)} %copy-done.81) | copy-start | bytes 6148
  493.8 31.7 %copy-start.85 = (f32[2,256]{1,0:T(2,128)S(1)}, f32[2,256]{1,0:T(2,128)}, u32[]{:S(2)}) copy-start(f32[2,256]{1,0:T(2,128)} %copy-done.84) | copy-start | bytes 6148
  536.2 61.4 %all-reduce.32.cloned.1.call-start = ((), (), s32[]{:S(2)}) async-start(), calls=%async_computation.22 | async-start | bytes 1572864 | tf_op jit(solution)/shard_map/psum | solution.py:57
  562.7 235.9 %all-reduce.34.cloned.1.call-start = ((), (), s32[]{:S(2)}) async-start(), calls=%async_computation.23 | async-start | bytes 10616832 | tf_op jit(solution)/shard_map/psum | solution.py:338
  564.8 36.0 %copy-start.110 = (bf16[2,384]{1,0:T(2,128)(2,1)S(1)}, bf16[2,384]{1,0:T(2,128)(2,1)}, u32[]{:S(2)}) copy-start(bf16[2,384]{1,0:T(2,128)(2,1)} %multiply_reduce_fusion.1) | copy-start | bytes 4612
  564.8 36.1 %copy-start.109 = (bf16[2,384]{1,0:T(2,128)(2,1)S(1)}, bf16[2,384]{1,0:T(2,128)(2,1)}, u32[]{:S(2)}) copy-start(bf16[2,384]{1,0:T(2,128)(2,1)} %get-tuple-element.112) | copy-start | bytes 4612
  564.8 36.1 %copy-start.108 = (bf16[2,384]{1,0:T(2,128)(2,1)S(1)}, bf16[2,384]{1,0:T(2,128)(2,1)}, u32[]{:S(2)}) copy-start(bf16[2,384]{1,0:T(2,128)(2,1)} %get-tuple-element.39) | copy-start | bytes 4612
  564.8 36.1 %copy-start.106 = (bf16[2,384]{1,0:T(2,128)(2,1)S(1)}, bf16[2,384]{1,0:T(2,128)(2,1)}, u32[]{:S(2)}) copy-start(bf16[2,384]{1,0:T(2,128)(2,1)} %multiply_reduce_fusion) | copy-start | bytes 4612
  564.8 36.7 %copy-start.93 = (bf16[2,192]{1,0:T(2,128)(2,1)S(1)}, bf16[2,192]{1,0:T(2,128)(2,1)}, u32[]{:S(2)}) copy-start(bf16[2,192]{1,0:T(2,128)(2,1)} %param.14) | copy-start | bytes 2308
  565.8 36.2 %copy-start.10 = (bf16[2,256,384]{2,1,0:T(8,128)(2,1)S(1)}, bf16[2,256,384]{2,1,0:T(8,128)(2,1)}, u32[]{:S(2)}) copy-start(bf16[2,256,384]{2,1,0:T(8,128)(2,1)} %param.15) | copy-start | bytes 1179652
  565.8 36.2 %copy-start.60 = (f32[2,384]{1,0:T(2,128)S(1)}, f32[2,384]{1,0:T(2,128)}, u32[]{:S(2)}) copy-start(f32[2,384]{1,0:T(2,128)} %copy-done.59) | copy-start | bytes 9220
  565.8 36.2 %copy-start.102 = (f32[384]{0:T(512)S(1)}, f32[384]{0:T(512)}, u32[]{:S(2)}) copy-start(f32[384]{0:T(512)} %get-tuple-element.61) | copy-start | bytes 4612
  609.1 31.9 %copy-start.94 = (bf16[2,192]{1,0:T(2,128)(2,1)S(1)}, bf16[2,192]{1,0:T(2,128)(2,1)}, u32[]{:S(2)}) copy-start(bf16[2,192]{1,0:T(2,128)(2,1)} %param.14) | copy-start | bytes 2308
  609.1 32.5 %copy-start.11 = (bf16[2,256,384]{2,1,0:T(8,128)(2,1)S(1)}, bf16[2,256,384]{2,1,0:T(8,128)(2,1)}, u32[]{:S(2)}) copy-start(bf16[2,256,384]{2,1,0:T(8,128)(2,1)} %get-tuple-element.83) | copy-start | bytes 1179652
  609.1 32.4 %copy-start.89 = (f32[2,256]{1,0:T(2,128)S(1)}, f32[2,256]{1,0:T(2,128)}, u32[]{:S(2)}) copy-start(f32[2,256]{1,0:T(2,128)} %copy-done.87) | copy-start | bytes 6148
  609.1 32.4 %copy-start.92 = (f32[2,256]{1,0:T(2,128)S(1)}, f32[2,256]{1,0:T(2,128)}, u32[]{:S(2)}) copy-start(f32[2,256]{1,0:T(2,128)} %copy-done.90) | copy-start | bytes 6148
  (92 other events, 419.0 us)
Sparse Core Ops, SparseCore 0:
  32.3 22.0 reduce-scatter.8
  63.3 32.5 all-reduce.19
  105.3 26.0 reduce-scatter.10
  145.9 32.6 all-reduce.21
  187.8 21.7 reduce-scatter.12
  218.8 32.6 all-reduce.23
  254.3 26.0 reduce-scatter.16
  283.3 26.0 reduce-scatter.14
  326.3 32.6 all-reduce.25
  373.2 13.1 reduce-scatter.18
  400.9 32.6 all-reduce.27
  448.3 28.6 reduce-scatter.20
  492.1 33.4 all-reduce.29
  536.3 13.1 reduce-scatter.22
  562.8 34.7 all-reduce.31
  605.0 193.5 all-reduce.33
where the time goes:
time: 818 us; the launch traced here: 816 us
  waiting for transfers between devices  513 us (63%)
  blocking collectives  157 us (19%)
  other arithmetic  73.9 us (9%)
  matrix products  44.7 us (5%)
  between operations  15.1 us (2%)
  local copies, waits for them, and re-layouts  10.2 us (1%)
    psum x7, waiting for transfers between devices, over_col(): return lax.psum(term.astype(jnp.bfloat16), 'col').astype(jnp.float32)  221 us
    psum x1, waiting for transfers between devices, local(): lax.psum(stacked[0].astype(jnp.bfloat16), 'dp').astype(jnp.float32)  156 us
    reduce_scatter x8, waiting for transfers between devices, over_row(): lax.psum_scatter(term_maker(jnp.int32(0), latents // lax.axis_size('row')...  136 us
    all_gather x8, blocking collectives, to_all_rows(): return lax.all_gather(pieces, 'row', axis=0, tiled=True)  80.9 us
    psum x8, blocking collectives, row_moments(): first_sum, second_sum = lax.psum((first_sum, second_sum), 'row')  41.6 us
    psum x1, blocking collectives, local(): lax.psum(stacked[1].astype(jnp.bfloat16), 'dp').astype(jnp.float32)  21.7 us
  transfers between devices with their start and end apart: 16, of which 16 were waited for; matrix products, arithmetic and copies ran while one was open for 5% of the time, Pallas kernels for 0%

commit v1 on v0

v1 whole, which is shorter than its diff:
```python
import functools

import jax
import jax.numpy as jnp
from jax import lax
from jax.experimental import pallas as pl
from jax.experimental.pallas import tpu as pltpu
from jax.sharding import PartitionSpec as P

HEAD = 64
EPSILON = 1e-06
MESH = pl.DeviceIdType.MESH
F32 = jnp.float32
BF16 = jnp.bfloat16


def silu_plain(values):
    return values * jax.nn.sigmoid(values)


def dot(a, b, ca=1, cb=0):
    return lax.dot_general(a, b, (((ca,), (cb,)), ((), ())), preferred_element_type=F32)


def gelu_parts(u):
    inner = 0.7978845608028654 * (u + 0.044715 * u * u * u)
    t = jnp.tanh(inner)
    value = 0.5 * u * (1.0 + t)
    slope = 0.5 * (1.0 + t) + 0.5 * u * (1.0 - t * t) * 0.7978845608028654 * (
        1.0 + 3.0 * 0.044715 * u * u
    )
    return value, slope


def gelu_value(u):
    return 0.5 * u * (1.0 + jnp.tanh(0.7978845608028654 * (u + 0.044715 * u * u * u)))


def gelu_slope(u):
    return gelu_parts(u)[1]


def layer_norm(v):
    average = jnp.mean(v, axis=-1, keepdims=True)
    square = jnp.mean(v * v, axis=-1, keepdims=True)
    inverse = lax.rsqrt(square - average * average + EPSILON)
    return (v - average) * inverse, inverse


def norm_back(g, normed, inverse):
    first = jnp.mean(g, axis=-1, keepdims=True)
    second = jnp.mean(g * normed, axis=-1, keepdims=True)
    return inverse * (g - first - normed * second)


def col_sum(v):
    return jnp.sum(v, axis=0, keepdims=True)


def softmax_parts(q, k):
    scores = dot(q, k, 1, 1) * HEAD ** (-0.5)
    expos = jnp.exp(scores - jnp.max(scores, axis=-1, keepdims=True))
    return expos / jnp.sum(expos, axis=-1, keepdims=True)


def block_kernel(
    layers, n_row, n_col, tokens, cotangent, mod_part, w_qkv, w_out, w_up, w_down,
    b_qkv, b_out, b_up, b_down,
    result, tok_grad, g_qkv, g_out, g_up, g_down, small,
    wq, wo, wu, wd, tok, cot, modbuf, mod, ag, rs, rs_send, own_send, gat,
    proj, mix, attn, n1, i1, n2, i2, before, act, feed, stream,
    gq_s, go_s, gu_s, gd_s, gq_r, go_r, gu_r, gd_r, res_send, res_r,
    ph_send, ph_recv, w_local, w_send, w_recv, g_send, g_recv, p_send, p_recv, t_local, t_send, t_recv,
):
    r = lax.axis_index("row")
    c = lax.axis_index("col")
    group = n_row * n_col
    peers = []
    for k in range(1, group):
        idx = lax.rem(r * n_col + c + k, group)
        peers.append((k, idx // n_col, lax.rem(idx, n_col)))
    barrier = pltpu.get_barrier_semaphore()
    for _, pr, pc in peers:
        pl.semaphore_signal(barrier, inc=1, device_id={"row": pr, "col": pc}, device_id_type=MESH)
    pl.semaphore_wait(barrier, group - 1)
    other = n_row - 1 - r
    mate = {"row": other, "col": c}
    chunk = tokens.shape[1] // n_col
    full = tokens.shape[1]
    pending = []

    def remote(src, dst, ss, rsem, where):
        cp = pltpu.make_async_remote_copy(
            src_ref=src, dst_ref=dst, send_sem=ss, recv_sem=rsem, device_id=where, device_id_type=MESH
        )
        cp.start()
        pending.append(cp)
        return cp

    mod_copies = []
    for k, pr, pc in peers:
        mod_copies.append(
            remote(mod_part.at[pr], modbuf.at[r, c], p_send.at[0, k], p_recv.at[0, k], {"row": pr, "col": pc})
        )
    rows = pl.ds(pl.multiple_of(c * chunk, chunk), chunk)
    tok_copies = []
    for n, (src, dst) in enumerate(((tokens, tok), (cotangent, cot))):
        if n == 0:
            tok_copies.append(remote(src.at[other, rows], dst.at[r], t_send.at[n], t_recv.at[n], mate))
        here = pltpu.make_async_copy(src.at[r, rows], dst.at[r], t_local.at[n])
        here.start()
        tok_copies.append(here)
    weights = [(w_qkv, wq), (w_out, wo), (w_up, wu), (w_down, wd)]
    w_copies = {}
    for l in range(layers):
        for n, (src, dst) in enumerate(weights):
            s = l * 4 + n
            far = remote(src.at[l], dst.at[l, r], w_send.at[s], w_recv.at[s], mate)
            here = pltpu.make_async_copy(src.at[l], dst.at[l, r], w_local.at[s])
            here.start()
            w_copies[(l, n)] = (far, here)
    cot_far = remote(cotangent.at[other, rows], cot.at[r], t_send.at[1], t_recv.at[1], mate)

    def need(l, n):
        far, here = w_copies[(l, n)]
        far.wait_recv()
        here.wait()

    def gather_start(ph, value):
        ag[ph, c] = value
        out = []
        for k in range(1, n_col):
            where = {"row": r, "col": lax.rem(c + k, n_col)}
            out.append(remote(ag.at[ph, c], ag.at[ph, c], ph_send.at[2 * ph, k], ph_recv.at[2 * ph, k], where))
        return out

    def gather_end(ph, copies):
        for cp in copies:
            cp.wait_recv()
        return ag[ph].reshape(full, ag.shape[-1])

    def gathered(ph):
        return ag[ph].reshape(full, ag.shape[-1])

    def scatter_start(ph, parts):
        half = parts[0].shape[1]
        for j, part in enumerate(parts):
            rs_send[ph, :, :, j * half:(j + 1) * half] = part.astype(BF16).reshape(n_col, chunk, half)
        out = []
        for k in range(1, n_col):
            to = lax.rem(c + k, n_col)
            out.append(
                remote(
                    rs_send.at[ph, to], rs.at[ph, k - 1], ph_send.at[2 * ph + 1, k],
                    ph_recv.at[2 * ph + 1, k], {"row": r, "col": to},
                )
            )
        return out

    def scatter_end(ph, copies):
        total = rs_send[ph, c].astype(F32)
        for k, cp in enumerate(copies):
            cp.wait_recv()
            total = total + rs[ph, k].astype(F32)
        return total

    def modrow(l, slot):
        return mod[l * 6 + slot:l * 6 + slot + 1, :]

    width = n_row * tokens.shape[2]
    half = tokens.shape[2]
    heads_w = mix.shape[-1]
    n_heads = heads_w // HEAD

    def spread(ph, value, slot, buf_out):
        for j in range(n_row):
            res_send[slot, j] = value[:, j * half:(j + 1) * half]
        out = []
        for k, pr, pc in peers:
            out.append(
                remote(
                    res_send.at[slot, pr], res_r.at[slot, r, c], p_send.at[1 + slot, k],
                    p_recv.at[1 + slot, k], {"row": pr, "col": pc},
                )
            )
        res_r[slot, r, c] = res_send[slot, r]
        return out

    def spread_end(copies, slot, out_ref):
        for cp in copies:
            cp.wait_recv()
        out_ref[...] = res_r[slot]

    modbuf[r, c] = mod_part[r]
    for cp in mod_copies:
        cp.wait_recv()
    for j in range(n_row):
        total = modbuf[j, 0]
        for k in range(1, n_col):
            total = total + modbuf[j, k]
        mod[:, j * half:(j + 1) * half] = total
    tok_copies[0].wait_recv()
    tok_copies[1].wait()
    tok_copies[2].wait()
    x = jnp.concatenate([tok[j] for j in range(n_row)], axis=1).astype(F32)

    for l in range(layers):
        normed, inverse = layer_norm(x)
        n1[l] = normed
        i1[l] = inverse
        hidden = (normed * (1.0 + modrow(l, 1)) + modrow(l, 0)).astype(BF16)
        ph = 4 * l
        copies = gather_start(ph, hidden)
        need(l, 0)
        hid = gather_end(ph, copies)
        p = dot(hid[:, :half], wq[l, 0]) + dot(hid[:, half:], wq[l, 1])
        proj[l] = (p + b_qkv[l:l + 1, :]).astype(BF16)
        for h in range(n_heads):
            lo = h * HEAD
            q = proj[l, :, lo:lo + HEAD]
            kk = proj[l, :, heads_w + lo:heads_w + lo + HEAD]
            vv = proj[l, :, 2 * heads_w + lo:2 * heads_w + lo + HEAD]
            soft = softmax_parts(q, kk).astype(BF16)
            mix[l, :, lo:lo + HEAD] = dot(soft, vv).astype(BF16)
        need(l, 1)
        m = mix[l]
        copies = scatter_start(ph, [dot(m, wo[l, j]) for j in range(n_row)])
        attention = scatter_end(ph, copies) + b_out[l:l + 1, :]
        attn[l] = attention
        x = x + modrow(l, 2) * attention
        stream[l] = x
        normed, inverse = layer_norm(x)
        n2[l] = normed
        i2[l] = inverse
        hidden = (normed * (1.0 + modrow(l, 4)) + modrow(l, 3)).astype(BF16)
        ph = 4 * l + 1
        copies = gather_start(ph, hidden)
        need(l, 2)
        hid = gather_end(ph, copies)
        u = dot(hid[:, :half], wu[l, 0]) + dot(hid[:, half:], wu[l, 1]) + b_up[l:l + 1, :]
        before[l] = u
        act[l] = gelu_value(u).astype(BF16)
        need(l, 3)
        a = act[l]
        copies = scatter_start(ph, [dot(a, wd[l, j]) for j in range(n_row)])
        fo = scatter_end(ph, copies) + b_down[l:l + 1, :]
        feed[l] = fo
        x = x + modrow(l, 5) * fo
    res_copies = spread(0, x.astype(BF16), 0, result)
    cot_far.wait_recv()
    g = jnp.concatenate([cot[j] for j in range(n_row)], axis=1).astype(F32)

    grads = [(gq_s, gq_r, g_qkv), (go_s, go_r, g_out), (gu_s, gu_r, g_up), (gd_s, gd_r, g_down)]
    g_copies = []

    def grad_send(l, n):
        src, dst, out = grads[n]
        s = l * 4 + n
        cp = remote(src.at[l, other], dst.at[l], g_send.at[s], g_recv.at[s], mate)
        g_copies.append((l, n, cp))

    small[...] = jnp.zeros_like(small)
    for l in reversed(range(layers)):
        ph = 4 * l + 2
        gf = (g * modrow(l, 5)).astype(BF16)
        copies = gather_start(ph, gf)
        small[l * 6 + 5:l * 6 + 6, :] = col_sum(g * feed[l])
        small[12 + l:13 + l, :] = col_sum(gf.astype(F32))
        slope = gelu_slope(before[l])
        gf_all = gather_end(ph, copies)
        ga = dot(gf_all[:, :half], wd[l, 0], 1, 1) + dot(gf_all[:, half:], wd[l, 1], 1, 1)
        gb = (ga * slope).astype(BF16)
        copies = scatter_start(ph, [dot(gb, wu[l, j], 1, 1) for j in range(n_row)])
        a = act[l]
        for j in range(n_row):
            gd_s[l, j] = dot(a, gf_all[:, j * half:(j + 1) * half], 0, 0).astype(BF16)
        grad_send(l, 3)
        small[16 + l:17 + l, :] = col_sum(gb.astype(F32))
        hid2 = gathered(4 * l + 1)
        for j in range(n_row):
            gu_s[l, j] = dot(hid2[:, j * half:(j + 1) * half], gb, 0, 0).astype(BF16)
        grad_send(l, 2)
        gh = scatter_end(ph, copies)
        normed = n2[l]
        gm = g + norm_back(gh * (1.0 + modrow(l, 4)), normed, i2[l])
        gattn = (gm * modrow(l, 2)).astype(BF16)
        ph = 4 * l + 3
        copies = gather_start(ph, gattn)
        small[l * 6 + 4:l * 6 + 5, :] = col_sum(gh * normed)
        small[l * 6 + 3:l * 6 + 4, :] = col_sum(gh)
        small[l * 6 + 2:l * 6 + 3, :] = col_sum(gm * attn[l])
        small[14 + l:15 + l, :] = col_sum(gattn.astype(F32))
        ga_all = gather_end(ph, copies)
        gmix = (
            dot(ga_all[:, :half], wo[l, 0], 1, 1) + dot(ga_all[:, half:], wo[l, 1], 1, 1)
        ).astype(BF16)
        scale = HEAD ** (-0.5)
        for h in range(n_heads):
            lo = h * HEAD
            q = proj[l, :, lo:lo + HEAD]
            kk = proj[l, :, heads_w + lo:heads_w + lo + HEAD]
            vv = proj[l, :, 2 * heads_w + lo:2 * heads_w + lo + HEAD]
            gh_ = gmix[:, lo:lo + HEAD]
            soft = softmax_parts(q, kk)
            gs = dot(gh_, vv, 1, 1)
            gsc = (soft * (gs - jnp.sum(soft * gs, axis=-1, keepdims=True))).astype(BF16)
            gat[:, lo:lo + HEAD] = (dot(gsc, kk) * scale).astype(BF16)
            gat[:, heads_w + lo:heads_w + lo + HEAD] = (dot(gsc, q, 0, 0) * scale).astype(BF16)
            gat[:, 2 * heads_w + lo:2 * heads_w + lo + HEAD] = dot(soft.astype(BF16), gh_, 0, 0).astype(BF16)
        gp = gat[...]
        copies = scatter_start(ph, [dot(gp, wq[l, j], 1, 1) for j in range(n_row)])
        hid1 = gathered(4 * l)
        for j in range(n_row):
            gq_s[l, j] = dot(hid1[:, j * half:(j + 1) * half], gp, 0, 0).astype(BF16)
        grad_send(l, 0)
        m = mix[l]
        for j in range(n_row):
            go_s[l, j] = dot(m, ga_all[:, j * half:(j + 1) * half], 0, 0).astype(BF16)
        grad_send(l, 1)
        small[18 + l:19 + l, :gp.shape[1]] = col_sum(gp.astype(F32))
        gh = scatter_end(ph, copies)
        normed = n1[l]
        small[l * 6 + 1:l * 6 + 2, :] = col_sum(gh * normed)
        small[l * 6:l * 6 + 1, :] = col_sum(gh)
        g = gm + norm_back(gh * (1.0 + modrow(l, 1)), normed, i1[l])
    tg_copies = spread(1, g.astype(BF16), 1, tok_grad)
    for l, n, cp in g_copies:
        src, dst, out = grads[n]
        cp.wait_recv()
        out[l] = (src[l, r].astype(F32) + dst[l].astype(F32)).astype(BF16)
    spread_end(res_copies, 0, result)
    spread_end(tg_copies, 1, tok_grad)
    for cp in pending:
        cp.wait_send()


def run_blocks(n_row, n_col, tokens, cotangent, mod_part, w_qkv, w_out, w_up, w_down, b_qkv, b_out, b_up, b_down):
    layers, half, qkv_w = w_qkv.shape
    full = tokens.shape[1]
    chunk = full // n_col
    width = half * n_row
    head_w = w_out.shape[1]
    hid = w_up.shape[2]
    any_spec = pl.BlockSpec(memory_space=pl.ANY)
    vmem = pl.BlockSpec(memory_space=pltpu.VMEM)
    group = n_row * n_col
    out_shape = (
        jax.ShapeDtypeStruct((n_row, n_col, chunk, half), BF16),
        jax.ShapeDtypeStruct((n_row, n_col, chunk, half), BF16),
        jax.ShapeDtypeStruct((layers, half, qkv_w), BF16),
        jax.ShapeDtypeStruct((layers, head_w, half), BF16),
        jax.ShapeDtypeStruct((layers, half, hid), BF16),
        jax.ShapeDtypeStruct((layers, hid, half), BF16),
        jax.ShapeDtypeStruct((24, width), F32),
    )
    dma = pltpu.SemaphoreType.DMA
    v = pltpu.VMEM
    phases = 4 * layers
    scratch = [
        v((layers, n_row, half, qkv_w), BF16),
        v((layers, n_row, head_w, half), BF16),
        v((layers, n_row, half, hid), BF16),
        v((layers, n_row, hid, half), BF16),
        v((n_row, chunk, half), BF16),
        v((n_row, chunk, half), BF16),
        v((n_row, n_col) + mod_part.shape[1:], F32),
        v((mod_part.shape[1], width), F32),
        v((phases, n_col, chunk, width), BF16),
        v((phases, n_col - 1, chunk, width), BF16),
        v((phases, n_col, chunk, width), BF16),
        v((16, 128), BF16),
        v((full, qkv_w), BF16),
        v((layers, full, qkv_w), BF16),
        v((layers, full, head_w), BF16),
        v((layers, chunk, width), F32),
        v((layers, chunk, width), F32),
        v((layers, chunk, 1), F32),
        v((layers, chunk, width), F32),
        v((layers, chunk, 1), F32),
        v((layers, full, hid), F32),
        v((layers, full, hid), BF16),
        v((layers, chunk, width), F32),
        v((layers, chunk, width), F32),
        v((layers, n_row, half, qkv_w), BF16),
        v((layers, n_row, head_w, half), BF16),
        v((layers, n_row, half, hid), BF16),
        v((layers, n_row, hid, half), BF16),
        v((layers, half, qkv_w), BF16),
        v((layers, head_w, half), BF16),
        v((layers, half, hid), BF16),
        v((layers, hid, half), BF16),
        v((2, n_row, chunk, half), BF16),
        v((2, n_row, n_col, chunk, half), BF16),
        dma((2 * phases, n_col)),
        dma((2 * phases, n_col)),
        dma((4 * layers,)),
        dma((4 * layers,)),
        dma((4 * layers,)),
        dma((4 * layers,)),
        dma((4 * layers,)),
        dma((3, group)),
        dma((3, group)),
        dma((2,)),
        dma((2,)),
        dma((2,)),
    ]
    return pl.pallas_call(
        functools.partial(block_kernel, layers, n_row, n_col),
        out_shape=out_shape,
        in_specs=[any_spec, any_spec, vmem, any_spec, any_spec, any_spec, any_spec, vmem, vmem, vmem, vmem],
        out_specs=tuple([vmem] * 7),
        scratch_shapes=scratch,
        compiler_params=pltpu.CompilerParams(
            collective_id=0, has_side_effects=True, vmem_limit_bytes=58 * 1024 * 1024
        ),
        name="blocks",
    )(tokens, cotangent, mod_part, w_qkv, w_out, w_up, w_down, b_qkv, b_out, b_up, b_down)


def local(n_dp, n_row, n_col, tokens, condition, cotangent, w_ada, b_ada, w_qkv, b_qv, w_out, b_out,
          up_weight, up_bias, down_weight, down_bias):
    layers = w_ada.shape[0]
    half = tokens.shape[2]
    latents = tokens.shape[0]
    r = lax.axis_index("row")
    c = lax.axis_index("col")
    d = lax.axis_index("dp")
    cond_float = condition.astype(F32)
    cond_low = silu_plain(cond_float).astype(BF16)
    cond_all = lax.all_gather(cond_low, "dp", axis=0, tiled=True)
    part = jnp.einsum("lc,nckd->lnkd", cond_low, w_ada, preferred_element_type=F32)
    part = part + jnp.where(c == 0, b_ada.astype(F32), 0.0)[None]
    part = jnp.pad(part.reshape(latents, layers * 6, half), ((0, 0), (0, 4), (0, 0)))
    bq = b_qv.astype(F32)
    b_qkv = jnp.concatenate([bq[:, 0], jnp.zeros_like(bq[:, 0]), bq[:, 1]], axis=1)
    row_bias = lax.all_gather(jnp.stack([b_out, down_bias]), "row", axis=2, tiled=True).astype(F32)
    q_w = w_qkv.shape[3]
    res, tg, g_qkv, g_out, g_up, g_down, small = run_blocks(
        n_row, n_col, tokens, cotangent, part, w_qkv.reshape(layers, half, 3 * q_w), w_out, up_weight,
        down_weight, b_qkv, row_bias[0], up_bias.astype(F32), row_bias[1],
    )
    g_qkv, g_out, g_up, g_down = [
        t.astype(F32) for t in lax.psum((g_qkv, g_out, g_up, g_down), "dp")
    ]
    summed = lax.psum(small[:16], "col")
    table = jnp.concatenate([summed, small[16:20]], axis=0).astype(BF16)
    table = lax.all_gather(table, ("dp", "row"), axis=0)
    mine = lax.dynamic_slice_in_dim(table[:, :16], r * half, half, axis=2)
    gmod = mine[:, :12].reshape(-1, layers, 6, half)
    w_ada_grad = jnp.einsum("lc,lnkd->nckd", cond_all, gmod, preferred_element_type=F32)
    b_ada_grad = jnp.sum(gmod, axis=0, dtype=F32)
    own = lax.dynamic_slice_in_dim(gmod, d * latents, latents, axis=0)
    cond_term = lax.psum(jnp.einsum("lnkd,nckd->lc", own, w_ada, preferred_element_type=F32), "row")
    condition_grad = jax.vjp(silu_plain, cond_float)[1](cond_term)[0].astype(BF16)
    vec = jnp.sum(mine[:, 12:16], axis=0, dtype=F32)
    rest = jnp.sum(table[:, 16:20], axis=0, dtype=F32)
    b_qkv_g = rest[2:4, : 3 * q_w].reshape(layers, 3, q_w)
    return (
        res.reshape(tokens.shape),
        tg.reshape(tokens.shape),
        condition_grad,
        w_ada_grad,
        b_ada_grad,
        g_qkv.reshape(w_qkv.shape),
        jnp.stack([b_qkv_g[:, 0], b_qkv_g[:, 2]], axis=1),
        g_out,
        vec[2:4],
        g_up,
        rest[0:2],
        g_down,
        vec[0:2],
    )


def solution(mesh):
    in_specs = (
        P("dp", None, "row"),
        P("dp", "col"),
        P("dp", None, "row"),
        P(None, "col", None, "row"),
        P(None, None, "row"),
        P(None, "row", None, "col"),
        P(None, None, "col"),
        P(None, "col", "row"),
        P(None, "row"),
        P(None, "row", "col"),
        P(None, "col"),
        P(None, "col", "row"),
        P(None, "row"),
    )
    out_specs = (
        P("dp", None, "row"),
        P("dp", None, "row"),
        P("dp", "col"),
        P(None, "col", None, "row"),
        P(None, None, "row"),
        P(None, "row", None, "col"),
        P(None, None, "col"),
        P(None, "col", "row"),
        P(None, "row"),
        P(None, "row", "col"),
        P(None, "col"),
        P(None, "col", "row"),
        P(None, "row"),
    )
    sizes = [mesh.shape[a] for a in ("dp", "row", "col")]
    return jax.shard_map(
        functools.partial(local, *sizes), mesh=mesh, in_specs=in_specs, out_specs=out_specs, check_vma=False
    )
```

time: 818 us -> 369 us (0.45)
  waiting for transfers between devices: 513 us -> 70.3 us
  Pallas kernels: 0 us -> 190 us
  blocking collectives: 157 us -> 67.2 us
  other arithmetic: 73.9 us -> 13 us
  matrix products: 44.7 us -> 4.02 us
    psum x8 -> x1, waiting for transfers between devices: 377 us -> 70.3 us  [local(): lax.psum((g_qkv, g_out, g_up, g_down), 'dp')]
    pallas_call x0 -> x1, Pallas kernels: none -> 190 us  [run_blocks(): pl.pallas_call(functools.partial(block_kernel, layers, n_row, n_col), out...]
    reduce_scatter x8 -> x0, waiting for transfers between devices: 136 us -> none  [over_row(): lax.psum_scatter(term_maker(jnp.int32(0), latents // lax.axis_size('row')...]
    psum x10 -> x2, blocking collectives: 76.5 us -> 18.5 us  [the longest x1 13.6 us: local(): summed = lax.psum(small[:16], 'col')]
    dot_general x41 -> x3, matrix products: 44.7 us -> 4.02 us  [the longest x1 2.46 us: local(): jnp.einsum('lc,lnkd->nckd', cond_all, gmod, preferred_element_type=F32)]
    all_gather x8 -> x3, blocking collectives: 80.9 us -> 48.6 us  [the longest x1 33.1 us: local(): table = lax.all_gather(table, ('dp', 'row'), axis=0)]
    reduce_sum x24 -> x3, other arithmetic: 32.2 us -> 0.11 us  [the longest x1 0.05 us: local(): b_ada_grad = jnp.sum(gmod, axis=0, dtype=F32)]
    convert_element_type x24 -> x6, other arithmetic: 26.6 us -> 7.02 us  [the longest x3 5.05 us: local(): t.astype(F32)]
  transfers between devices with their start and end apart: 16 -> 1, of which waited for: 16 -> 1; matrix products, arithmetic and copies ran while one was open for 5% -> 2% of each run, Pallas kernels for 0% -> 0%
where the time goes in v1:
time: 369 us; the launch traced here: 368 us
  Pallas kernels  190 us (51%)
  waiting for transfers between devices  70.3 us (19%)
  blocking collectives  67.2 us (18%)
  between operations  14.2 us (4%)
  other arithmetic  13 us (4%)
  local copies, waits for them, and re-layouts  9.34 us (3%)
  matrix products  4.02 us (1%)
    pallas_call x1, Pallas kernels, run_blocks(): pl.pallas_call(functools.partial(block_kernel, layers, n_row, n_col), out...  190 us
    psum x1, waiting for transfers between devices, local(): lax.psum((g_qkv, g_out, g_up, g_down), 'dp')  70.3 us
    all_gather x1, blocking collectives, local(): table = lax.all_gather(table, ('dp', 'row'), axis=0)  33.1 us
    psum x1, blocking collectives, local(): summed = lax.psum(small[:16], 'col')  13.6 us
    all_gather x1, blocking collectives, local(): cond_all = lax.all_gather(cond_low, 'dp', axis=0, tiled=True)  10.3 us
  transfers between devices with their start and end apart: 1, of which 1 were waited for; matrix products, arithmetic and copies ran while one was open for 2% of the time, Pallas kernels for 0%

profile of v1, /device:TPU:0, one launch (start us, length us, event | category | flops | bytes accessed | tf_op | source)
XLA Modules:
  0.0 368.1 jit_solution(7109524755878299757)
XLA Ops:
  7.2 0.0 copy-start
  7.2 0.0 copy-start.3
  7.2 0.0 all-reduce.4.cloned.1.call-start
  7.3 0.9 pad_maximum_fusion.3
  8.1 5.2 %all_gather.10 = bf16[2,2,768]{2,1,0:T(2,128)(2,1)S(1)} all-gather(bf16[2,2,384]{2,1,0:T(2,128)(2,1)S(1)} %pad_maximum_fusion.3), channel_id=1, replica_groups=mesh['dp'=4,'row'=2,'col'=4] {'row'}, dimensions={2}, use_global_device_ids=true | all-gather | bytes 9216 | tf_op jit(solution)/shard_map/all_gather | solution.py:436
  13.3 0.7 copy_convert_fusion
  14.0 0.6 slice_bitcast_fusion
  14.6 1.3 convert_element_type.56.b_up
  15.9 0.7 convert_select_fusion
  16.6 0.0 copy-done
  16.6 1.0 convolution_add_fusion
  17.7 0.0 copy-done.3
  17.7 1.3 copy.46.w_qkv
  19.0 0.6 pad.4.mod_part
  19.6 0.1 pad.12.clone
  19.7 0.6 pad_maximum_fusion.1.b_qkv
  20.3 190.0 %blocks.1 = (bf16[2,4,64,384]{3,2,1,0:T(8,128)(2,1)}, bf16[2,4,64,384]{3,2,1,0:T(8,128)(2,1)}, bf16[2,384,576]{2,1,0:T(8,128)(2,1)}, bf16[2,192,384]{2,1,0:T(8,1...) custom-call(bf16[2,256,384]{2,1,0:T(8,128)(2,1)} %tokens.1, ...), custom_call_target="tpu_custom_call" | custom-call | tf_op jit(solution)/shard_map/blocks/pallas_call | solution.py:407
  210.4 2.2 copy.50
  212.6 0.0 copy-start.6
  212.6 0.0 all-reduce.4.cloned.1.call-update
  212.6 0.0 copy-start.7
  212.6 0.8 copy-done.6
  213.4 13.6 %psum.42 = bf16[16,768]{1,0:T(8,128)(2,1)S(1)} all-reduce(f32[16,768]{1,0:T(8,128)S(1)} %slice.53), channel_id=1, replica_groups=mesh['dp'=4,'row'=2,'col'=4] {'col'}, use_global_device_ids=true, to_apply=%region_0.1 | all-reduce | flops 12288 | bytes 73728 | tf_op jit(solution)/shard_map/psum | solution.py:445
  227.1 33.1 %all_gather.11 = bf16[8,20,768]{2,1,0:T(8,128)(2,1)S(1)} all-gather(bf16[1,20,768]{2,1,0:T(8,128)(2,1)S(1)} %pad_maximum_fusion), channel_id=1, replica_groups=mesh['dp'=4,'row'=2,'col'=4] {'dp','row'}, dimensions={0}, use_global_device_ids=true | all-gather | bytes 276480 | tf_op jit(solution)/shard_map/all_gather | solution.py:447
  260.2 0.6 slice.76
  260.8 0.1 reshape.90
  260.9 0.1 convert_reduce_fusion
  261.0 0.6 copy.51
  261.6 0.6 fusion.2
  262.2 4.9 %psum.43 = f32[2,192]{1,0:T(2,128)S(1)} all-reduce(f32[2,192]{1,0:T(2,128)S(1)} %fusion.2), channel_id=1, replica_groups=mesh['dp'=4,'row'=2,'col'=4] {'row'}, use_global_device_ids=true, to_apply=%region_1.2 | all-reduce | flops 384 | bytes 3072 | tf_op jit(solution)/shard_map/psum | solution.py:453
  267.1 0.0 copy-done.7
  267.1 0.6 fusion.16
  267.7 10.3 %all-gather = bf16[4,2,192]{2,1,0:T(2,128)(2,1)S(1)} all-gather(bf16[1,2,192]{2,1,0:T(2,128)(2,1)S(1)} %get-tuple-element.67), channel_id=1, replica_groups=mesh['dp'=4,'row'=2,'col'=4] {'dp'}, dimensions={0}, use_global_device_ids=true | all-gather | bytes 3840 | tf_op jit(solution)/shard_map/all_gather | solution.py:430
  278.1 0.6 pad_maximum_fusion.2
  278.7 0.1 constant_dynamic-slice_fusion.2
  278.8 0.6 fusion.20
  279.4 2.5 convolution_bitcast_fusion
  281.8 70.3 %all-reduce.4.cloned.1.call-done = (bf16[2,384,3,192]{1,3,2,0:T(8,128)(2,1)}, bf16[2,192,384]{2,1,0:T(8,128)(2,1)}, bf16[2,384,768]{2,1,0:T(8,128)(2,1)}, bf16[2,768,384]{2,1,0:T(8,128)(2,1)}) async-done(((bf16[2,384,3,192]{1,3,2,0:T(8,128)(2,1)}, bf16[2,192,384]{2,1,0:T(8,128)(2,1)}, bf16[2,384,768]{2,1,0:T(8,128)(2,1)}, bf16[2,768,384]{2,1,0:T(8,128)(2,1)}), (bf16[2,384,3,192]{1,3,2,0:T(8,128)(2,1)}, ...) | async-done | bytes 3538960 | tf_op jit(solution)/shard_map/psum | solution.py:443
  352.1 1.9 convert_element_type.60
  354.0 2.5 reshape.89
  356.5 0.0 copy-done.2
  356.5 1.6 convert_element_type.62
  358.1 0.1 copy-done.1
  358.2 1.6 convert_element_type.63
  359.8 0.0 copy-done.5
  359.8 0.7 copy.75
  360.5 0.0 copy-done.4
  360.5 0.7 copy.76
  (20 shorter events, 0.2 us)
Async XLA Ops:
  7.2 9.5 %copy-start = (bf16[2,192,6,384]{3,1,2,0:T(8,128)(2,1)S(1)}, bf16[2,192,6,384]{3,1,2,0:T(8,128)(2,1)}, u32[]{:S(2)}) copy-start(bf16[2,192,6,384]{3,1,2,0:T(8,128)(2,1)} %param.16) | copy-start | bytes 5308420
  7.2 10.5 %copy-start.3 = (bf16[2,384,3,192]{1,3,2,0:T(8,128)(2,1)S(1)}, bf16[2,384,3,192]{1,3,2,0:T(8,128)(2,1)}, u32[]{:S(2)}) copy-start(bf16[2,384,3,192]{1,3,2,0:T(8,128)(2,1)} %param.18) | copy-start | bytes 2654212
  7.2 344.9 %all-reduce.4.cloned.1.call-start = ((), (), s32[]{:S(2)}) async-start(), calls=%async_computation | async-start | bytes 7077888 | tf_op jit(solution)/shard_map/psum | solution.py:443
  212.6 0.9 copy-start.6
  212.6 54.5 %copy-start.7 = (bf16[2,192]{1,0:T(2,128)(2,1)S(1)}, bf16[2,192]{1,0:T(2,128)(2,1)}, u32[]{:S(2)}) copy-start(bf16[2,192]{1,0:T(2,128)(2,1)} %param.14) | copy-start | bytes 2308
  352.1 4.4 %copy-start.2 = (bf16[2,384,768]{2,1,0:T(8,128)(2,1)S(1)}, bf16[2,384,768]{2,1,0:T(8,128)(2,1)}, u32[]{:S(2)}) copy-start(bf16[2,384,768]{2,1,0:T(8,128)(2,1)} %get-tuple-element.55) | copy-start | bytes 3538948
  356.5 1.7 copy-start.1
  358.2 1.6 copy-start.5
  358.2 2.3 copy-start.4
Sparse Core Ops, SparseCore 0:
  212.7 139.3 all-reduce.3

commit v2 on v1

--- a/solution.py
+++ b/solution.py
@@ -64,17 +64,22 @@
 
 
 def block_kernel(
-    layers, n_row, n_col, tokens, cotangent, mod_part, w_qkv, w_out, w_up, w_down,
+    layers, n_dp, n_row, n_col, tokens, cotangent, mod_part, cond, w_qkv, w_out, w_up, w_down,
     b_qkv, b_out, b_up, b_down,
-    result, tok_grad, g_qkv, g_out, g_up, g_down, small,
+    result, tok_grad, g_qkv, g_out, g_up, g_down, table,
+    small, col_r, tab_s,
     wq, wo, wu, wd, tok, cot, modbuf, mod, ag, rs, rs_send, own_send, gat,
     proj, mix, attn, n1, i1, n2, i2, before, act, feed, stream,
-    gq_s, go_s, gu_s, gd_s, gq_r, go_r, gu_r, gd_r, res_send, res_r,
+    gq_s, go_s, gu_s, gd_s, gq_r, go_r, gu_r, gd_r, zq, zo, zu, zd, yq, yo, yu, yd, xq, xo, xu, xd, res_send, res_r,
     ph_send, ph_recv, w_local, w_send, w_recv, g_send, g_recv, p_send, p_recv, t_local, t_send, t_recv,
+    z_send, z_recv, c_send, c_recv, d_send, d_recv,
 ):
     r = lax.axis_index("row")
     c = lax.axis_index("col")
+    d = lax.axis_index("dp")
     group = n_row * n_col
+    tree = n_dp == 4
+    line = n_dp * n_row
     peers = []
     for k in range(1, group):
         idx = lax.rem(r * n_col + c + k, group)
@@ -82,7 +87,11 @@
     barrier = pltpu.get_barrier_semaphore()
     for _, pr, pc in peers:
         pl.semaphore_signal(barrier, inc=1, device_id={"row": pr, "col": pc}, device_id_type=MESH)
-    pl.semaphore_wait(barrier, group - 1)
+    for k in range(1, n_dp):
+        for j in range(n_row):
+            where = {"dp": lax.rem(d + k, n_dp), "row": jnp.int32(j)}
+            pl.semaphore_signal(barrier, inc=1, device_id=where, device_id_type=MESH)
+    pl.semaphore_wait(barrier, group - 1 + n_row * (n_dp - 1))
     other = n_row - 1 - r
     mate = {"row": other, "col": c}
     chunk = tokens.shape[1] // n_col
@@ -259,6 +268,80 @@
         cp = remote(src.at[l, other], dst.at[l], g_send.at[s], g_recv.at[s], mate)
         g_copies.append((l, n, cp))
 
+    near = [zq, zo, zu, zd]
+    across = [yq, yo, yu, yd]
+    sums = [xq, xo, xu, xd]
+    inner = (d == 1) | (d == 2)
+    leaf = jnp.logical_not(inner)
+    pair = {"dp": d + 1 - 2 * lax.rem(d, 2)}
+    facing = {"dp": 3 - d}
+
+    def hop(l, n, step):
+        s = l * 4 + n
+        src, dst, where = (
+            (sums[n], near[n], pair), (sums[n], across[n], facing), (near[n], near[n], pair)
+        )[step]
+        return pltpu.make_async_remote_copy(
+            src_ref=src.at[l], dst_ref=dst.at[l], send_sem=z_send.at[s, step], recv_sem=z_recv.at[s, step],
+            device_id=where, device_id_type=MESH,
+        )
+
+    def add_row(l, n, cp):
+        src, dst, out = grads[n]
+        cp.wait_recv()
+        total = (src[l, r].astype(F32) + dst[l].astype(F32)).astype(BF16)
+        if not tree:
+            out[l] = total
+            return
+        sums[n][l] = total
+
+        @pl.when(leaf)
+        def _():
+            hop(l, n, 0).start()
+
+    def add_near(l, n, cp):
+        @pl.when(inner)
+        def _():
+            hop(l, n, 0).wait_recv()
+            sums[n][l] = (sums[n][l].astype(F32) + near[n][l].astype(F32)).astype(BF16)
+            hop(l, n, 1).start()
+
+    def add_across(l, n, cp):
+        @pl.when(inner)
+        def _():
+            hop(l, n, 1).wait_recv()
+            total = (sums[n][l].astype(F32) + across[n][l].astype(F32)).astype(BF16)
+            near[n][l] = total
+            hop(l, n, 2).start()
+            grads[n][2][l] = total
+
+    def finish(l, n, cp):
+        @pl.when(leaf)
+        def _():
+            hop(l, n, 2).wait_recv()
+            grads[n][2][l] = near[n][l]
+            hop(l, n, 0).wait_send()
+
+        @pl.when(inner)
+        def _():
+            hop(l, n, 1).wait_send()
+            hop(l, n, 2).wait_send()
+
+    stages = [add_row, add_near, add_across, finish] if tree else [add_row]
+    queue = []
+
+    def advance():
+        while len(queue) < len(g_copies):
+            queue.append(0)
+        moves = []
+        for i, (l, n, cp) in enumerate(g_copies):
+            if queue[i] < len(stages):
+                moves.append((stages[queue[i]], l, n, cp))
+                queue[i] += 1
+        for f, l, n, cp in moves:
+            f(l, n, cp)
+        return len(moves)
+
     small[...] = jnp.zeros_like(small)
     for l in reversed(range(layers)):
         ph = 4 * l + 2
@@ -267,6 +350,7 @@
         small[l * 6 + 5:l * 6 + 6, :] = col_sum(g * feed[l])
         small[12 + l:13 + l, :] = col_sum(gf.astype(F32))
         slope = gelu_slope(before[l])
+        advance()
         gf_all = gather_end(ph, copies)
         ga = dot(gf_all[:, :half], wd[l, 0], 1, 1) + dot(gf_all[:, half:], wd[l, 1], 1, 1)
         gb = (ga * slope).astype(BF16)
@@ -309,6 +393,7 @@
             gat[:, 2 * heads_w + lo:2 * heads_w + lo + HEAD] = dot(soft.astype(BF16), gh_, 0, 0).astype(BF16)
         gp = gat[...]
         copies = scatter_start(ph, [dot(gp, wq[l, j], 1, 1) for j in range(n_row)])
+        advance()
         hid1 = gathered(4 * l)
         for j in range(n_row):
             gq_s[l, j] = dot(hid1[:, j * half:(j + 1) * half], gp, 0, 0).astype(BF16)
@@ -324,17 +409,36 @@
         small[l * 6:l * 6 + 1, :] = col_sum(gh)
         g = gm + norm_back(gh * (1.0 + modrow(l, 1)), normed, i1[l])
     tg_copies = spread(1, g.astype(BF16), 1, tok_grad)
-    for l, n, cp in g_copies:
-        src, dst, out = grads[n]
+    out = []
+    for k in range(1, n_col):
+        where = {"row": r, "col": lax.rem(c + k, n_col)}
+        out.append(remote(small.at[:16], col_r.at[k - 1], c_send.at[k], c_recv.at[k], where))
+    advance()
+    total = small[:16]
+    for k, cp in enumerate(out):
         cp.wait_recv()
-        out[l] = (src[l, r].astype(F32) + dst[l].astype(F32)).astype(BF16)
+        total = total + col_r[k]
+    low = jnp.concatenate([small[16:24], cond[r]], axis=0)
+    tab_s[...] = jnp.concatenate([total, low], axis=0).astype(BF16)
+    me = d * n_row + r
+    out = []
+    for k in range(1, line):
+        to = lax.rem(me + k, line)
+        where = {"dp": to // n_row, "row": lax.rem(to, n_row)}
+        out.append(remote(tab_s, table.at[me], d_send.at[k], d_recv.at[k], where))
+    table[me] = tab_s[...]
+    advance()
+    for cp in out:
+        cp.wait_recv()
+    while advance():
+        pass
     spread_end(res_copies, 0, result)
     spread_end(tg_copies, 1, tok_grad)
     for cp in pending:
         cp.wait_send()
 
 
-def run_blocks(n_row, n_col, tokens, cotangent, mod_part, w_qkv, w_out, w_up, w_down, b_qkv, b_out, b_up, b_down):
+def run_blocks(n_dp, n_row, n_col, tokens, cotangent, mod_part, cond, w_qkv, w_out, w_up, w_down, b_qkv, b_out, b_up, b_down):
     layers, half, qkv_w = w_qkv.shape
     full = tokens.shape[1]
     chunk = full // n_col
@@ -351,12 +455,16 @@
         jax.ShapeDtypeStruct((layers, head_w, half), BF16),
         jax.ShapeDtypeStruct((layers, half, hid), BF16),
         jax.ShapeDtypeStruct((layers, hid, half), BF16),
-        jax.ShapeDtypeStruct((24, width), F32),
+        jax.ShapeDtypeStruct((n_dp * n_row, 32, width), BF16),
     )
     dma = pltpu.SemaphoreType.DMA
     v = pltpu.VMEM
     phases = 4 * layers
+    grads = [(layers, half, qkv_w), (layers, head_w, half), (layers, half, hid), (layers, hid, half)]
     scratch = [
+        v((24, width), F32),
+        v((n_col - 1, 16, width), F32),
+        v((32, width), BF16),
         v((layers, n_row, half, qkv_w), BF16),
         v((layers, n_row, head_w, half), BF16),
         v((layers, n_row, half, hid), BF16),
@@ -389,6 +497,7 @@
         v((layers, head_w, half), BF16),
         v((layers, half, hid), BF16),
         v((layers, hid, half), BF16),
+        *[v(g, BF16) for g in grads * 3],
         v((2, n_row, chunk, half), BF16),
         v((2, n_row, n_col, chunk, half), BF16),
         dma((2 * phases, n_col)),
@@ -403,18 +512,24 @@
         dma((2,)),
         dma((2,)),
         dma((2,)),
+        dma((4 * layers, 3)),
+        dma((4 * layers, 3)),
+        dma((n_col,)),
+        dma((n_col,)),
+        dma((n_dp * n_row,)),
+        dma((n_dp * n_row,)),
     ]
     return pl.pallas_call(
-        functools.partial(block_kernel, layers, n_row, n_col),
+        functools.partial(block_kernel, layers, n_dp, n_row, n_col),
         out_shape=out_shape,
-        in_specs=[any_spec, any_spec, vmem, any_spec, any_spec, any_spec, any_spec, vmem, vmem, vmem, vmem],
+        in_specs=[any_spec, any_spec, vmem, vmem, any_spec, any_spec, any_spec, any_spec, vmem, vmem, vmem, vmem],
         out_specs=tuple([vmem] * 7),
         scratch_shapes=scratch,
         compiler_params=pltpu.CompilerParams(
             collective_id=0, has_side_effects=True, vmem_limit_bytes=58 * 1024 * 1024
         ),
         name="blocks",
-    )(tokens, cotangent, mod_part, w_qkv, w_out, w_up, w_down, b_qkv, b_out, b_up, b_down)
+    )(tokens, cotangent, mod_part, cond, w_qkv, w_out, w_up, w_down, b_qkv, b_out, b_up, b_down)
 
 
 def local(n_dp, n_row, n_col, tokens, condition, cotangent, w_ada, b_ada, w_qkv, b_qv, w_out, b_out,
@@ -427,24 +542,25 @@
     d = lax.axis_index("dp")
     cond_float = condition.astype(F32)
     cond_low = silu_plain(cond_float).astype(BF16)
-    cond_all = lax.all_gather(cond_low, "dp", axis=0, tiled=True)
     part = jnp.einsum("lc,nckd->lnkd", cond_low, w_ada, preferred_element_type=F32)
     part = part + jnp.where(c == 0, b_ada.astype(F32), 0.0)[None]
     part = jnp.pad(part.reshape(latents, layers * 6, half), ((0, 0), (0, 4), (0, 0)))
+    cond_rows = jnp.pad(
+        cond_low.astype(F32)[:, None], ((0, 0), (0, 7), (0, n_row * half - condition.shape[1]))
+    )
     bq = b_qv.astype(F32)
     b_qkv = jnp.concatenate([bq[:, 0], jnp.zeros_like(bq[:, 0]), bq[:, 1]], axis=1)
     row_bias = lax.all_gather(jnp.stack([b_out, down_bias]), "row", axis=2, tiled=True).astype(F32)
     q_w = w_qkv.shape[3]
-    res, tg, g_qkv, g_out, g_up, g_down, small = run_blocks(
-        n_row, n_col, tokens, cotangent, part, w_qkv.reshape(layers, half, 3 * q_w), w_out, up_weight,
+    res, tg, g_qkv, g_out, g_up, g_down, table = run_blocks(
+        n_dp, n_row, n_col, tokens, cotangent, part, cond_rows, w_qkv.reshape(layers, half, 3 * q_w), w_out, up_weight,
         down_weight, b_qkv, row_bias[0], up_bias.astype(F32), row_bias[1],
     )
-    g_qkv, g_out, g_up, g_down = [
-        t.astype(F32) for t in lax.psum((g_qkv, g_out, g_up, g_down), "dp")
-    ]
-    summed = lax.psum(small[:16], "col")
-    table = jnp.concatenate([summed, small[16:20]], axis=0).astype(BF16)
-    table = lax.all_gather(table, ("dp", "row"), axis=0)
+    sums = (g_qkv, g_out, g_up, g_down)
+    if n_dp != 4:
+        sums = lax.psum(sums, "dp")
+    g_qkv, g_out, g_up, g_down = [t.astype(F32) for t in sums]
+    cond_all = table[:, 24, : cond_low.shape[1]]
     mine = lax.dynamic_slice_in_dim(table[:, :16], r * half, half, axis=2)
     gmod = mine[:, :12].reshape(-1, layers, 6, half)
     w_ada_grad = jnp.einsum("lc,lnkd->nckd", cond_all, gmod, preferred_element_type=F32)

time: 369 us -> 293 us (0.79)
  waiting for transfers between devices: 70.3 us -> 0 us
  Pallas kernels: 190 us -> 255 us
  blocking collectives: 67.2 us -> 10.2 us
  between operations: 14.2 us -> 0.78 us
    psum x1 -> x0, waiting for transfers between devices: 70.3 us -> none  [local(): lax.psum((g_qkv, g_out, g_up, g_down), 'dp')]
    pallas_call x1, Pallas kernels: 190 us -> 255 us  [run_blocks(): pl.pallas_call(functools.partial(block_kernel, layers, n_dp, n_row, n_col...]
    all_gather x2 -> x0, blocking collectives: 43.4 us -> none  [the longest x1 33.1 us: local(): table = lax.all_gather(table, ('dp', 'row'), axis=0)]
    psum x1 -> x0, blocking collectives: 13.6 us -> none  [local(): summed = lax.psum(small[:16], 'col')]
  transfers between devices with their start and end apart: 1 -> 0, of which waited for: 1 -> 0; matrix products, arithmetic and copies ran while one was open for 2% -> 0% of each run, Pallas kernels for 0% -> 0%
where the time goes in v2:
time: 293 us; the launch traced here: 292 us
  Pallas kernels  255 us (87%)
  other arithmetic  11.7 us (4%)
  local copies, waits for them, and re-layouts  10.4 us (4%)
  blocking collectives  10.2 us (3%)
  matrix products  4.02 us (1%)
    pallas_call x1, Pallas kernels, run_blocks(): pl.pallas_call(functools.partial(block_kernel, layers, n_dp, n_row, n_col...  255 us

profile of v2, /device:TPU:0, one launch (start us, length us, event | category | flops | bytes accessed | tf_op | source)
XLA Modules:
  0.0 292.5 jit_solution(7900036072738449824)
XLA Ops:
  0.6 0.0 copy-start
  0.7 0.0 copy-start.3
  0.7 0.8 fusion.16
  1.5 0.1 pad.18.clone
  1.6 0.7 pad_maximum_fusion.2
  2.3 5.2 %all_gather.3 = bf16[2,2,768]{2,1,0:T(2,128)(2,1)S(1)} all-gather(bf16[2,2,384]{2,1,0:T(2,128)(2,1)S(1)} %pad_maximum_fusion.2), channel_id=1, replica_groups=mesh['dp'=4,'row'=2,'col'=4] {'row'}, dimensions={2}, use_global_device_ids=true | all-gather | bytes 9216 | tf_op jit(solution)/shard_map/all_gather | solution.py:553
  7.5 0.7 copy_convert_fusion
  8.2 0.6 pad_maximum_fusion.b_qkv
  8.8 0.6 slice_bitcast_fusion
  9.5 1.3 convert_element_type.51.b_up
  10.7 0.7 convert_select_fusion
  11.5 0.0 copy-done
  11.5 1.0 convolution_add_fusion
  12.5 0.6 pad.10.mod_part
  13.1 0.6 pad_convert_fusion.cond
  13.8 0.0 copy-done.3
  13.8 1.3 copy.38.w_qkv
  15.1 255.5 %blocks.1 = (bf16[2,4,64,384]{3,2,1,0:T(8,128)(2,1)}, bf16[2,4,64,384]{3,2,1,0:T(8,128)(2,1)}, bf16[2,384,576]{2,1,0:T(8,128)(2,1)}, bf16[2,192,384]{2,1,0:T(8,1...) custom-call(bf16[2,256,384]{2,1,0:T(8,128)(2,1)} %tokens.1, ...), custom_call_target="tpu_custom_call" | custom-call | tf_op jit(solution)/shard_map/blocks/pallas_call | solution.py:522
  270.5 0.0 copy-start.7
  270.6 0.0 copy-start.6
  270.6 0.8 slice.51
  271.4 0.9 convert_reduce_fusion.1
  272.3 0.9 slice.49
  273.3 0.6 slice.68
  273.9 0.1 reshape.59
  273.9 0.6 pad_maximum_fusion.1
  274.5 0.1 convert_reduce_fusion.2
  274.7 0.6 copy.43
  275.3 0.6 fusion.20
  275.9 0.6 fusion.2
  276.5 4.9 %psum.7 = f32[2,192]{1,0:T(2,128)S(1)} all-reduce(f32[2,192]{1,0:T(2,128)S(1)} %fusion.2), channel_id=1, replica_groups=mesh['dp'=4,'row'=2,'col'=4] {'row'}, use_global_device_ids=true, to_apply=%region_0.1 | all-reduce | flops 384 | bytes 3072 | tf_op jit(solution)/shard_map/psum | solution.py:569
  281.4 0.0 copy-done.7
  281.4 0.6 fusion.14
  282.0 0.0 copy-done.6
  282.0 0.0 copy-start.2
  282.0 0.9 convert_element_type.55
  282.9 2.4 copy.42
  285.3 0.0 copy-done.2
  285.3 0.0 copy-start.1
  285.3 1.6 convert_element_type.57
  286.9 0.1 copy-done.1
  287.0 1.6 convert_element_type.58
  288.5 0.0 copy-start.5
  288.5 2.5 convolution_bitcast_fusion
  291.0 0.0 copy-done.5
  291.0 0.7 copy.62
  291.7 0.0 copy-done.4
  291.7 0.7 copy.63
  (12 shorter events, 0.1 us)
Async XLA Ops:
  0.6 10.8 %copy-start = (bf16[2,192,6,384]{3,1,2,0:T(8,128)(2,1)S(1)}, bf16[2,192,6,384]{3,1,2,0:T(8,128)(2,1)}, u32[]{:S(2)}) copy-start(bf16[2,192,6,384]{3,1,2,0:T(8,128)(2,1)} %param.16) | copy-start | bytes 5308420
  0.7 13.1 %copy-start.3 = (bf16[2,384,3,192]{1,3,2,0:T(8,128)(2,1)S(1)}, bf16[2,384,3,192]{1,3,2,0:T(8,128)(2,1)}, u32[]{:S(2)}) copy-start(bf16[2,384,3,192]{1,3,2,0:T(8,128)(2,1)} %param.18) | copy-start | bytes 2654212
  270.5 10.9 %copy-start.7 = (bf16[2,192]{1,0:T(2,128)(2,1)S(1)}, bf16[2,192]{1,0:T(2,128)(2,1)}, u32[]{:S(2)}) copy-start(bf16[2,192]{1,0:T(2,128)(2,1)} %param.14) | copy-start | bytes 2308
  270.6 11.4 %copy-start.6 = (bf16[2,192,384]{2,1,0:T(8,128)(2,1)S(1)}, bf16[2,192,384]{2,1,0:T(8,128)(2,1)}, u32[]{:S(2)}) copy-start(bf16[2,192,384]{2,1,0:T(8,128)(2,1)} %get-tuple-element.24) | copy-start | bytes 884740
  282.0 3.3 %copy-start.2 = (bf16[2,384,768]{2,1,0:T(8,128)(2,1)S(1)}, bf16[2,384,768]{2,1,0:T(8,128)(2,1)}, u32[]{:S(2)}) copy-start(bf16[2,384,768]{2,1,0:T(8,128)(2,1)} %get-tuple-element.25) | copy-start | bytes 3538948
  285.3 1.7 copy-start.1
  288.5 2.5 copy-start.5
  288.5 3.2 %copy-start.4 = (bf16[2,4,64,384]{3,2,1,0:T(8,128)(2,1)S(1)}, bf16[2,4,64,384]{3,2,1,0:T(8,128)(2,1)}, u32[]{:S(2)}) copy-start(bf16[2,4,64,384]{3,2,1,0:T(8,128)(2,1)} %get-tuple-element.21) | copy-start | bytes 1179652

commit v3 on v2

--- a/solution.py
+++ b/solution.py
@@ -65,7 +65,7 @@
 
 def block_kernel(
     layers, n_dp, n_row, n_col, tokens, cotangent, mod_part, cond, w_qkv, w_out, w_up, w_down,
-    b_qkv, b_out, b_up, b_down,
+    b_qkv, b_up,
     result, tok_grad, g_qkv, g_out, g_up, g_down, table,
     small, col_r, tab_s,
     wq, wo, wu, wd, tok, cot, modbuf, mod, ag, rs, rs_send, own_send, gat,
@@ -234,7 +234,7 @@
         need(l, 1)
         m = mix[l]
         copies = scatter_start(ph, [dot(m, wo[l, j]) for j in range(n_row)])
-        attention = scatter_end(ph, copies) + b_out[l:l + 1, :]
+        attention = scatter_end(ph, copies) + mod[12 + l:13 + l, :]
         attn[l] = attention
         x = x + modrow(l, 2) * attention
         stream[l] = x
@@ -252,7 +252,7 @@
         need(l, 3)
         a = act[l]
         copies = scatter_start(ph, [dot(a, wd[l, j]) for j in range(n_row)])
-        fo = scatter_end(ph, copies) + b_down[l:l + 1, :]
+        fo = scatter_end(ph, copies) + mod[12 + layers + l:13 + layers + l, :]
         feed[l] = fo
         x = x + modrow(l, 5) * fo
     res_copies = spread(0, x.astype(BF16), 0, result)
@@ -262,11 +262,16 @@
     grads = [(gq_s, gq_r, g_qkv), (go_s, go_r, g_out), (gu_s, gu_r, g_up), (gd_s, gd_r, g_down)]
     g_copies = []
 
+    def span(n, p):
+        size = grads[n][1].shape[1] // 2
+        return pl.ds(p * size, size)
+
     def grad_send(l, n):
         src, dst, out = grads[n]
-        s = l * 4 + n
-        cp = remote(src.at[l, other], dst.at[l], g_send.at[s], g_recv.at[s], mate)
-        g_copies.append((l, n, cp))
+        for p in range(2):
+            s = (l * 4 + n) * 2 + p
+            cp = remote(src.at[l, other, span(n, p)], dst.at[l, span(n, p)], g_send.at[s], g_recv.at[s], mate)
+            g_copies.append((l, (n, p), cp))
 
     near = [zq, zo, zu, zd]
     across = [yq, yo, yu, yd]
@@ -276,56 +281,68 @@
     pair = {"dp": d + 1 - 2 * lax.rem(d, 2)}
     facing = {"dp": 3 - d}
 
-    def hop(l, n, step):
-        s = l * 4 + n
+    def hop(l, item, step):
+        n, p = item
+        s = (l * 4 + n) * 2 + p
         src, dst, where = (
             (sums[n], near[n], pair), (sums[n], across[n], facing), (near[n], near[n], pair)
         )[step]
         return pltpu.make_async_remote_copy(
-            src_ref=src.at[l], dst_ref=dst.at[l], send_sem=z_send.at[s, step], recv_sem=z_recv.at[s, step],
+            src_ref=src.at[l, span(n, p)], dst_ref=dst.at[l, span(n, p)], send_sem=z_send.at[s, step], recv_sem=z_recv.at[s, step],
             device_id=where, device_id_type=MESH,
         )
 
-    def add_row(l, n, cp):
+    def add_row(l, item, cp):
+        n, p = item
+        at = span(n, p)
         src, dst, out = grads[n]
         cp.wait_recv()
-        total = (src[l, r].astype(F32) + dst[l].astype(F32)).astype(BF16)
+        total = (src[l, r, at].astype(F32) + dst[l, at].astype(F32)).astype(BF16)
         if not tree:
-            out[l] = total
+            out[l, at] = total
             return
-        sums[n][l] = total
+        sums[n][l, at] = total
 
         @pl.when(leaf)
         def _():
-            hop(l, n, 0).start()
-
-    def add_near(l, n, cp):
+            hop(l, item, 0).start()
+
+    def add_near(l, item, cp):
+        n, p = item
+        at = span(n, p)
+
         @pl.when(inner)
         def _():
-            hop(l, n, 0).wait_recv()
-            sums[n][l] = (sums[n][l].astype(F32) + near[n][l].astype(F32)).astype(BF16)
-            hop(l, n, 1).start()
-
-    def add_across(l, n, cp):
+            hop(l, item, 0).wait_recv()
+            sums[n][l, at] = (sums[n][l, at].astype(F32) + near[n][l, at].astype(F32)).astype(BF16)
+            hop(l, item, 1).start()
+
+    def add_across(l, item, cp):
+        n, p = item
+        at = span(n, p)
+
         @pl.when(inner)
         def _():
-            hop(l, n, 1).wait_recv()
-            total = (sums[n][l].astype(F32) + across[n][l].astype(F32)).astype(BF16)
-            near[n][l] = total
-            hop(l, n, 2).start()
-            grads[n][2][l] = total
-
-    def finish(l, n, cp):
+            hop(l, item, 1).wait_recv()
+            total = (sums[n][l, at].astype(F32) + across[n][l, at].astype(F32)).astype(BF16)
+            near[n][l, at] = total
+            hop(l, item, 2).start()
+            grads[n][2][l, at] = total
+
+    def finish(l, item, cp):
+        n, p = item
+        at = span(n, p)
+
         @pl.when(leaf)
         def _():
-            hop(l, n, 2).wait_recv()
-            grads[n][2][l] = near[n][l]
-            hop(l, n, 0).wait_send()
+            hop(l, item, 2).wait_recv()
+            grads[n][2][l, at] = near[n][l, at]
+            hop(l, item, 0).wait_send()
 
         @pl.when(inner)
         def _():
-            hop(l, n, 1).wait_send()
-            hop(l, n, 2).wait_send()
+            hop(l, item, 1).wait_send()
+            hop(l, item, 2).wait_send()
 
     stages = [add_row, add_near, add_across, finish] if tree else [add_row]
     queue = []
@@ -403,6 +420,8 @@
             go_s[l, j] = dot(m, ga_all[:, j * half:(j + 1) * half], 0, 0).astype(BF16)
         grad_send(l, 1)
         small[18 + l:19 + l, :gp.shape[1]] = col_sum(gp.astype(F32))
+        if l == 0:
+            advance()
         gh = scatter_end(ph, copies)
         normed = n1[l]
         small[l * 6 + 1:l * 6 + 2, :] = col_sum(gh * normed)
@@ -438,7 +457,7 @@
         cp.wait_send()
 
 
-def run_blocks(n_dp, n_row, n_col, tokens, cotangent, mod_part, cond, w_qkv, w_out, w_up, w_down, b_qkv, b_out, b_up, b_down):
+def run_blocks(n_dp, n_row, n_col, tokens, cotangent, mod_part, cond, w_qkv, w_out, w_up, w_down, b_qkv, b_up):
     layers, half, qkv_w = w_qkv.shape
     full = tokens.shape[1]
     chunk = full // n_col
@@ -505,15 +524,15 @@
         dma((4 * layers,)),
         dma((4 * layers,)),
         dma((4 * layers,)),
-        dma((4 * layers,)),
-        dma((4 * layers,)),
+        dma((8 * layers,)),
+        dma((8 * layers,)),
         dma((3, group)),
         dma((3, group)),
         dma((2,)),
         dma((2,)),
         dma((2,)),
-        dma((4 * layers, 3)),
-        dma((4 * layers, 3)),
+        dma((8 * layers, 3)),
+        dma((8 * layers, 3)),
         dma((n_col,)),
         dma((n_col,)),
         dma((n_dp * n_row,)),
@@ -522,14 +541,14 @@
     return pl.pallas_call(
         functools.partial(block_kernel, layers, n_dp, n_row, n_col),
         out_shape=out_shape,
-        in_specs=[any_spec, any_spec, vmem, vmem, any_spec, any_spec, any_spec, any_spec, vmem, vmem, vmem, vmem],
+        in_specs=[any_spec, any_spec, vmem, vmem, any_spec, any_spec, any_spec, any_spec, vmem, vmem],
         out_specs=tuple([vmem] * 7),
         scratch_shapes=scratch,
         compiler_params=pltpu.CompilerParams(
             collective_id=0, has_side_effects=True, vmem_limit_bytes=58 * 1024 * 1024
         ),
         name="blocks",
-    )(tokens, cotangent, mod_part, cond, w_qkv, w_out, w_up, w_down, b_qkv, b_out, b_up, b_down)
+    )(tokens, cotangent, mod_part, cond, w_qkv, w_out, w_up, w_down, b_qkv, b_up)
 
 
 def local(n_dp, n_row, n_col, tokens, condition, cotangent, w_ada, b_ada, w_qkv, b_qv, w_out, b_out,
@@ -544,17 +563,18 @@
     cond_low = silu_plain(cond_float).astype(BF16)
     part = jnp.einsum("lc,nckd->lnkd", cond_low, w_ada, preferred_element_type=F32)
     part = part + jnp.where(c == 0, b_ada.astype(F32), 0.0)[None]
-    part = jnp.pad(part.reshape(latents, layers * 6, half), ((0, 0), (0, 4), (0, 0)))
+    biases = jnp.where(c == 0, jnp.concatenate([b_out, down_bias]).astype(F32), 0.0)
+    biases = jnp.broadcast_to(biases[None], (latents,) + biases.shape)
+    part = jnp.concatenate([part.reshape(latents, layers * 6, half), biases], axis=1)
     cond_rows = jnp.pad(
         cond_low.astype(F32)[:, None], ((0, 0), (0, 7), (0, n_row * half - condition.shape[1]))
     )
     bq = b_qv.astype(F32)
     b_qkv = jnp.concatenate([bq[:, 0], jnp.zeros_like(bq[:, 0]), bq[:, 1]], axis=1)
-    row_bias = lax.all_gather(jnp.stack([b_out, down_bias]), "row", axis=2, tiled=True).astype(F32)
     q_w = w_qkv.shape[3]
     res, tg, g_qkv, g_out, g_up, g_down, table = run_blocks(
         n_dp, n_row, n_col, tokens, cotangent, part, cond_rows, w_qkv.reshape(layers, half, 3 * q_w), w_out, up_weight,
-        down_weight, b_qkv, row_bias[0], up_bias.astype(F32), row_bias[1],
+        down_weight, b_qkv, up_bias.astype(F32),
     )
     sums = (g_qkv, g_out, g_up, g_down)
     if n_dp != 4:

time: 293 us -> 287 us (0.980)
  blocking collectives: 10.2 us -> 4.94 us
    all_gather x1 -> x0, blocking collectives: 5.22 us -> none  [local(): lax.all_gather(jnp.stack([b_out, down_bias]), 'row', axis=2, tiled=True)]
where the time goes in v3:
time: 287 us; the launch traced here: 286 us
  Pallas kernels  255 us (89%)
  other arithmetic  12.3 us (4%)
  local copies, waits for them, and re-layouts  9.13 us (3%)
  blocking collectives  4.94 us (2%)
  matrix products  4.02 us (1%)
    pallas_call x1, Pallas kernels, run_blocks(): pl.pallas_call(functools.partial(block_kernel, layers, n_dp, n_row, n_col...  255 us

profile of v3, /device:TPU:0, one launch (start us, length us, event | category | flops | bytes accessed | tf_op | source)
XLA Modules:
  0.0 286.5 jit_solution(14701839524053411882)
XLA Ops:
  0.6 0.0 copy-start
  0.7 0.0 copy-start.3
  0.7 0.8 fusion.16
  1.5 0.1 pad.11.clone
  1.6 0.7 copy_convert_fusion
  2.3 0.6 pad_maximum_fusion.1.b_qkv
  2.9 0.7 convert_select_fusion.1
  3.6 1.3 convert_element_type.53.b_up
  4.9 0.7 convert_select_fusion
  5.6 0.0 copy-done
  5.6 1.0 convolution_add_fusion
  6.7 0.6 pad_maximum_fusion.mod_part
  7.3 0.6 pad_convert_fusion.cond
  7.9 0.0 copy-done.3
  7.9 1.3 copy.38.w_qkv
  9.2 255.3 %blocks.1 = (bf16[2,4,64,384]{3,2,1,0:T(8,128)(2,1)}, bf16[2,4,64,384]{3,2,1,0:T(8,128)(2,1)}, bf16[2,384,576]{2,1,0:T(8,128)(2,1)}, bf16[2,192,384]{2,1,0:T(8,1...) custom-call(bf16[2,256,384]{2,1,0:T(8,128)(2,1)} %tokens.1, ...), custom_call_target="tpu_custom_call" | custom-call | tf_op jit(solution)/shard_map/blocks/pallas_call | solution.py:541
  264.6 0.0 copy-start.7
  264.6 0.0 copy-start.6
  264.6 0.8 slice.43
  265.4 0.9 convert_reduce_fusion.1
  266.3 0.9 slice.41
  267.3 0.6 slice.58
  267.9 0.1 reshape.75
  268.0 0.6 pad_maximum_fusion.2
  268.6 0.1 convert_reduce_fusion.2
  268.7 0.6 copy.43
  269.3 0.6 fusion.20
  269.9 0.6 fusion.2
  270.5 4.9 %psum.7 = f32[2,192]{1,0:T(2,128)S(1)} all-reduce(f32[2,192]{1,0:T(2,128)S(1)} %fusion.2), channel_id=1, replica_groups=mesh['dp'=4,'row'=2,'col'=4] {'row'}, use_global_device_ids=true, to_apply=%region_0.1 | all-reduce | flops 384 | bytes 3072 | tf_op jit(solution)/shard_map/psum | solution.py:589
  275.4 0.0 copy-done.7
  275.4 0.6 fusion.14
  276.0 0.0 copy-done.6
  276.0 0.0 copy-start.2
  276.0 0.9 convert_element_type.57
  276.9 2.4 copy.42
  279.3 0.0 copy-done.2
  279.3 0.0 copy-start.1
  279.3 1.6 convert_element_type.59
  280.9 0.1 copy-done.1
  281.0 1.6 convert_element_type.60
  282.5 0.0 copy-start.5
  282.5 0.0 copy-start.4
  282.5 2.5 convolution_bitcast_fusion
  285.0 0.0 copy-done.5
  285.0 0.7 copy.62
  285.7 0.0 copy-done.4
  285.7 0.7 copy.63
  (11 shorter events, 0.1 us)
Async XLA Ops:
  0.6 5.0 %copy-start = (bf16[2,192,6,384]{3,1,2,0:T(8,128)(2,1)S(1)}, bf16[2,192,6,384]{3,1,2,0:T(8,128)(2,1)}, u32[]{:S(2)}) copy-start(bf16[2,192,6,384]{3,1,2,0:T(8,128)(2,1)} %param.16) | copy-start | bytes 5308420
  0.7 7.3 %copy-start.3 = (bf16[2,384,3,192]{1,3,2,0:T(8,128)(2,1)S(1)}, bf16[2,384,3,192]{1,3,2,0:T(8,128)(2,1)}, u32[]{:S(2)}) copy-start(bf16[2,384,3,192]{1,3,2,0:T(8,128)(2,1)} %param.18) | copy-start | bytes 2654212
  264.6 10.9 %copy-start.7 = (bf16[2,192]{1,0:T(2,128)(2,1)S(1)}, bf16[2,192]{1,0:T(2,128)(2,1)}, u32[]{:S(2)}) copy-start(bf16[2,192]{1,0:T(2,128)(2,1)} %param.14) | copy-start | bytes 2308
  264.6 11.4 %copy-start.6 = (bf16[2,192,384]{2,1,0:T(8,128)(2,1)S(1)}, bf16[2,192,384]{2,1,0:T(8,128)(2,1)}, u32[]{:S(2)}) copy-start(bf16[2,192,384]{2,1,0:T(8,128)(2,1)} %get-tuple-element.24) | copy-start | bytes 884740
  276.0 3.3 %copy-start.2 = (bf16[2,384,768]{2,1,0:T(8,128)(2,1)S(1)}, bf16[2,384,768]{2,1,0:T(8,128)(2,1)}, u32[]{:S(2)}) copy-start(bf16[2,384,768]{2,1,0:T(8,128)(2,1)} %get-tuple-element.25) | copy-start | bytes 3538948
  279.3 1.7 copy-start.1
  282.5 2.5 copy-start.5
  282.5 3.2 %copy-start.4 = (bf16[2,4,64,384]{3,2,1,0:T(8,128)(2,1)S(1)}, bf16[2,4,64,384]{3,2,1,0:T(8,128)(2,1)}, u32[]{:S(2)}) copy-start(bf16[2,4,64,384]{3,2,1,0:T(8,128)(2,1)} %get-tuple-element.21) | copy-start | bytes 1179652
